TPU v7x, 32 devices: a whole 2x2x4 slice. The times are simulated.
32 devices in a mesh: gx: 8 (over z, y), gy: 4 (over x, core).
Axes of the slice: x: 2, y: 2, z: 4, core: 2. Of those that a mesh axis runs over, the one named last changes fastest.
Arguments:
- features: bfloat16 [32, 16, 512, 128], P('gx', 'gy'), may hold values from -6 to 6
- occupancy: int32 [32, 16], P('gx', 'gy'), may hold values from 0 to 1, as said below
- pair_offset: int32 [32, 16, 9], P('gx', 'gy'), may hold values from 0 to 27, as said below
- owner: int32 [32, 16], P('gx', 'gy'), may hold values from 0 to 7, as said below
- w_sub: bfloat16 [27, 128, 128], replicated, may hold values from -0.25 to 0.25
- w_down: bfloat16 [1024, 256], replicated, may hold values from -0.1875 to 0.1875
- cotangent: bfloat16 [32, 16, 64, 256], P('gx', 'gy'), may hold values from -6 to 6
Outputs:
- coarse: bfloat16 [32, 16, 64, 256], P('gx', 'gy')
- feature_grad: bfloat16 [32, 16, 512, 128], P('gx', 'gy')
- sub_grad: float32 [27, 128, 128], replicated
- down_grad: float32 [1024, 256], replicated
Inputs may be any that keep to these rules, and one draw needn't show every extreme that they name: `occupancy`: 1 where a column holds an occupied brick. `pair_offset`: entry k = 3 (dx + 1) + (dy + 1) of a column is 9 (dx + 1) + 3 (dy + 1) + (dz + 1) when that column and the neighbour column at dx, dy are both inside the grid and occupied and the neighbour's brick lies dz in -1..1 levels higher, else 27. The relation is symmetric: the neighbour's entry back is 27 exactly when this one is, and otherwise the two sum to 26. A column's coarse cell lies on device (owner, same gy index), at the same place within that device's 4 x 4 block as the column has in its own block. (owner minus the column's own gx index) modulo 8 depends only on the gy index and the place, so each device holds exactly one cell per place; each device sends exactly 2 columns to each device of its gx row, itself included.
All inputs are finite; a program needn't handle non-finite values.
Results may differ from a plain program's by a relative error of at most 0.005.
Values may be sent and summed in bfloat16 or wider, within the bound.
A program may use at most 192 MiB of HBM per device.

v0:
```python
import jax
import jax.numpy as jnp
from jax import lax
from jax.sharding import PartitionSpec as P

E = 8


NEIGHBOURS = [(-1, -1), (-1, 0), (-1, 1), (0, -1), (0, 0), (0, 1), (1, -1), (1, 0), (1, 1)]


def from_behind(value, axis, steps):
    count = lax.axis_size(axis)
    leading, last = (max(0, -steps), min(count, count - steps))
    return lax.ppermute(value, axis, [(source, source + steps) for source in range(leading, last)])


def with_halo(shard, sides, width):
    for axis, dim in sides:
        count, length = (lax.axis_size(axis), shard.shape[dim])
        up = [(i, (i + 1) % count) for i in range(count - 1)]
        down = [(j, i) for i, j in up]
        last = lax.slice_in_dim(shard, length - width, length, axis=dim)
        leading = lax.slice_in_dim(shard, 0, width, axis=dim)
        before = lax.ppermute(last, axis, up)
        after = lax.ppermute(leading, axis, down)
        shard = jnp.concatenate([before, shard, after], axis=dim)
    return shard


def bricks_to_patches(values):
    leading = values.shape[:-2]
    channels = values.shape[-1]
    half_edge = E // 2
    depth = len(leading)
    blocks = values.reshape(leading + (half_edge, 2, half_edge, 2, half_edge, 2, channels))
    layout = tuple(range(depth)) + (
        depth,
        depth + 2,
        depth + 4,
        depth + 1,
        depth + 3,
        depth + 5,
        depth + 6,
    )
    return blocks.transpose(layout).reshape(leading + (half_edge**3, 8 * channels))


def patches_to_bricks(values, channels):
    leading = values.shape[:-2]
    half_edge = E // 2
    depth = len(leading)
    blocks = values.reshape(leading + (half_edge, half_edge, half_edge, 2, 2, 2, channels))
    layout = tuple(range(depth)) + (
        depth,
        depth + 3,
        depth + 1,
        depth + 4,
        depth + 2,
        depth + 5,
        depth + 6,
    )
    return blocks.transpose(layout).reshape(leading + (E**3, channels))


def fold_rims(spread):
    from_below = from_behind(spread[-1].astype(jnp.bfloat16), "gx", 1).astype(jnp.float32)
    from_above = from_behind(spread[0].astype(jnp.bfloat16), "gx", -1).astype(jnp.float32)
    inner_rows = spread[1:-1]
    inner_rows = inner_rows.at[0].add(from_below).at[-1].add(from_above)
    from_left = from_behind(inner_rows[:, -1].astype(jnp.bfloat16), "gy", 1).astype(jnp.float32)
    from_right = from_behind(inner_rows[:, 0].astype(jnp.bfloat16), "gy", -1).astype(jnp.float32)
    core_block = inner_rows[:, 1:-1]
    return core_block.at[:, 0].add(from_left).at[:, -1].add(from_right)


def local(features, occupancy, pair_offset, owner, w_sub, w_down, cotangent):
    width_x, width_y, voxels, channels = features.shape
    bricks = width_x * width_y
    coarse_voxels = cotangent.shape[2]
    out_channels = cotangent.shape[3]
    brick_present = occupancy.astype(jnp.float32).reshape(bricks, 1, 1)
    masked = features * occupancy.astype(jnp.bfloat16)[:, :, None, None]
    flat_table = jnp.concatenate([w_sub, jnp.zeros((1, channels, channels), jnp.bfloat16)], 0)
    flat_table = flat_table.reshape(28, channels * channels)
    codes = jnp.arange(28, dtype=jnp.int32)
    offsets = pair_offset.reshape(bricks, 9)

    def select_weights(column):
        selector = (column[:, None] == codes[None, :]).astype(jnp.bfloat16)
        picked = jnp.dot(selector, flat_table, preferred_element_type=jnp.float32)
        return picked.astype(jnp.bfloat16).reshape(bricks, channels, channels)

    def window(values, stepping_x, stepping_y):
        part_block = values[
            1 + stepping_x : 1 + stepping_x + width_x, 1 + stepping_y : 1 + stepping_y + width_y
        ]
        return part_block.reshape(bricks, voxels, channels)

    def joined_windows(values):
        return jnp.concatenate(
            [window(values, stepping_x, stepping_y) for stepping_x, stepping_y in NEIGHBOURS], 2
        )

    extended = with_halo(masked, (("gx", 0), ("gy", 1)), 1)
    chosen = [select_weights(offsets[:, direction]) for direction in range(9)]
    stacked_weights = jnp.concatenate(chosen, 1)
    preact = jnp.einsum(
        "nho,nor->nhr",
        joined_windows(extended),
        stacked_weights,
        preferred_element_type=jnp.float32,
    )
    sigmoid_pre = jax.nn.sigmoid(preact)
    own_masked = masked.reshape(bricks, voxels, channels).astype(jnp.float32)
    hidden_features = (brick_present * (own_masked + preact * sigmoid_pre)).astype(jnp.bfloat16)
    brick_patches = bricks_to_patches(hidden_features).reshape(bricks * coarse_voxels, 8 * channels)
    shifted_rows = jnp.dot(brick_patches, w_down, preferred_element_type=jnp.float32).astype(
        jnp.bfloat16
    )
    shifted_rows = shifted_rows.reshape(bricks, coarse_voxels, out_channels)
    peer_count = lax.axis_size("gx")
    own_index = lax.axis_index("gx")
    targets = owner.reshape(bricks)
    places = jnp.arange(bricks, dtype=jnp.int32)
    send_order = jnp.argsort(targets * bricks + places)
    outgoing = shifted_rows[send_order].reshape(
        peer_count, bricks // peer_count, coarse_voxels, out_channels
    )
    incoming = lax.all_to_all(outgoing, "gx", split_axis=0, concat_axis=0, tiled=True)
    source = (2 * own_index - targets) % peer_count
    cell_order = jnp.argsort(source * bricks + places)
    coarse = jnp.zeros((bricks, coarse_voxels, out_channels), jnp.bfloat16)
    coarse = coarse.at[cell_order].set(incoming.reshape(bricks, coarse_voxels, out_channels))
    returning = cotangent.reshape(bricks, coarse_voxels, out_channels)[cell_order]
    returning = returning.reshape(peer_count, bricks // peer_count, coarse_voxels, out_channels)
    returned_all = lax.all_to_all(returning, "gx", split_axis=0, concat_axis=0, tiled=True)
    returned_rows = jnp.zeros((bricks, coarse_voxels, out_channels), jnp.bfloat16)
    returned_rows = returned_rows.at[send_order].set(
        returned_all.reshape(bricks, coarse_voxels, out_channels)
    )
    flat_returned = returned_rows.reshape(bricks * coarse_voxels, out_channels)
    down_grad = lax.dot_general(
        brick_patches, flat_returned, (((0,), (0,)), ((), ())), preferred_element_type=jnp.float32
    )
    patch_gradient = lax.dot_general(
        flat_returned, w_down, (((1,), (1,)), ((), ())), preferred_element_type=jnp.float32
    )
    hidden_gradient = patches_to_bricks(
        patch_gradient.reshape(bricks, coarse_voxels, 8 * channels), channels
    )
    slope_value = sigmoid_pre * (1.0 + preact * (1.0 - sigmoid_pre))
    pre_grad = (brick_present * hidden_gradient * slope_value).astype(jnp.bfloat16)
    sub_grad = jnp.zeros((28, channels * channels), jnp.float32)
    for direction, (stepping_x, stepping_y) in enumerate(NEIGHBOURS):
        outer = jnp.einsum(
            "bvc,bvd->bcd",
            window(extended, stepping_x, stepping_y),
            pre_grad,
            preferred_element_type=jnp.float32,
        )
        selector = (offsets[:, direction][:, None] == codes[None, :]).astype(jnp.float32)
        sub_grad = sub_grad + lax.dot_general(
            selector,
            outer.reshape(bricks, channels * channels),
            (((0,), (0,)), ((), ())),
            precision=lax.Precision.HIGHEST,
        )
    spread = jnp.zeros((width_x + 2, width_y + 2, voxels, channels), jnp.float32)
    for direction, (stepping_x, stepping_y) in enumerate(NEIGHBOURS):
        contrib = jnp.einsum(
            "bvd,bcd->bvc", pre_grad, chosen[direction], preferred_element_type=jnp.float32
        )
        contrib = contrib.reshape(width_x, width_y, voxels, channels)
        spread = spread + jnp.pad(
            contrib,
            ((1 + stepping_x, 1 - stepping_x), (1 + stepping_y, 1 - stepping_y), (0, 0), (0, 0)),
        )
    conv_grad = fold_rims(spread).reshape(bricks, voxels, channels)
    feature_grad = (brick_present * (hidden_gradient + conv_grad)).astype(jnp.bfloat16)
    totals = lax.psum((sub_grad[:27].reshape(27, channels, channels), down_grad), ("gx", "gy"))
    device_count = lax.axis_size("gx") * lax.axis_size("gy")
    return (
        coarse.reshape(width_x, width_y, coarse_voxels, out_channels),
        feature_grad.reshape(width_x, width_y, voxels, channels),
        totals[0] / device_count,
        totals[1] / device_count,
    )


def solution(mesh):
    in_specs = (
        P("gx", "gy", None, None),
        P("gx", "gy"),
        P("gx", "gy", None),
        P("gx", "gy"),
        P(),
        P(),
        P("gx", "gy", None, None),
    )
    out_specs = (P("gx", "gy", None, None), P("gx", "gy", None, None), P(), P())
    return jax.shard_map(local, mesh=mesh, in_specs=in_specs, out_specs=out_specs, check_vma=False)
```

profile of v0, /device:TPU:0, one launch (start us, length us, event | category | flops | bytes accessed | tf_op | source)
XLA Modules:
  0.0 381.5 jit_solution(750630268354857453)
XLA Ops:
  7.9 1.8 broadcast_multiply_fusion
  9.8 1.3 copy-done.1
  12.1 4.9 %collective-permute-start = (bf16[1,4,512,128]{3,2,1,0:T(8,128)(2,1)}, bf16[1,4,512,128]{3,2,1,0:T(8,128)(2,1)S(1)}, u32[]{:S(2)}, u32[]{:S(2)}) collective-permute-start(bf16[1,4,512,128]{3,2,1,0:T(8,128)(2,1)} %get-tuple-element.78), channel_id=1, source_target_pairs={{0,4},{4,8},{8,12},{12,16},{16,20},{20,24},{24,28},{1,5},{5,9},{9,... | collective-permute-start | bytes 1572872 | tf_op jit(solution)/shard_map/ppermute | solution.py:25
  17.0 1.3 collective-permute-start.1
  21.1 1.4 gather_fusion.1
  22.4 7.7 %all-to-all-start.1 = ((bf16[8,2,64,256]{3,2,1,0:T(8,128)(2,1)}), bf16[8,2,64,256]{3,2,1,0:T(8,128)(2,1)}, u32[]{:S(2)}, u32[]{:S(2)}) async-start(bf16[8,2,64,256]{3,2,1,0:T(8,128)(2,1)} %bitcast.26), calls=%async_computation.1 | async-start | bytes 1048576 | tf_op jit(solution)/shard_map/all_to_all | solution.py:137
  48.8 2.0 constant_dynamic-update-slice_fusion.12
  50.7 2.0 constant_dynamic-update-slice_fusion.11
  52.7 2.4 pad_maximum_fusion.3
  55.1 2.2 collective-permute-start.2
  57.3 1.7 collective-permute-start.3
  60.8 3.4 pad_maximum_fusion.1
  65.1 2.9 scatter_fusion.1
  68.0 1.3 copy.45
  70.1 4.2 %copy.46 = f32[16,4,2,4,2,4,2,128]{7,6,5,4,3,2,1,0:T(2,128)} copy(f32[16,4,2,4,2,4,2,128]{7,0,6,4,2,5,3,1:T(8,128)S(1)} %convolution_bitcast_fusion) | data formatting | bytes 8388608 | tf_op jit(solution)/shard_map/transpose | solution.py:63
  74.3 3.3 pad_maximum_fusion
  77.6 1.3 fusion.62
  79.3 2.8 copy-done.5
  87.4 6.5 %copy-done.48 = bf16[16,512,1152]{2,1,0:T(8,128)(2,1)} copy-done((bf16[16,512,1152]{2,1,0:T(8,128)(2,1)}, bf16[16,512,1152]{2,1,0:T(8,128)(2,1)S(1)}, u32[]{:S(2)}) %copy-start.48) | copy-done | bytes 18874392
  93.8 12.8 %multiply_convert_fusion.1 = (bf16[16,512,128]{2,1,0:T(8,128)(2,1)S(1)}, bf16[16,512,128]{2,1,0:T(8,128)(2,1)}) fusion(f32[16,512,128]{2,1,0:T(8,128)} %bitcast.246, f32[16]{0:T(128)S(1)} %mul.55, bf16[4,4,512,128]{3,2,1,0:T(8,128)(2,1)S(1)} %copy-done.2, bf16[16,512,1152]{2,1,0:T(8,128)(2,1)} %copy-done.48, ...), kind=kOutput, calls=%fused_computation.17 | convolution fusion | flops 2431647744 | bytes 34078784 | tf_op jit(solution)/shard_map/nho,nor->nhr/dot_general | solution.py:108
  106.6 2.4 fusion.76
  109.0 1.7 fusion.77
  110.8 1.7 fusion.78
  120.5 2.7 fusion.70
  123.2 2.7 fusion.71
  125.9 2.7 fusion.72
  128.6 2.7 fusion.73
  131.3 2.7 fusion.74
  134.4 2.7 fusion.75
  137.1 2.9 fusion.34
  139.9 2.9 fusion.12
  142.8 2.9 fusion.18
  145.7 2.8 fusion.21
  148.5 2.9 fusion.27
  151.4 2.9 fusion.15
  154.3 2.9 fusion.24
  157.2 13.1 %fusion.61 = (bf16[6,6,512,128]{3,2,1,0:T(8,128)(2,1)}, f32[6,6,512,128]{3,2,1,0:T(8,128)}) fusion(f32[4,4,512,128]{3,2,1,0:T(8,128)} %bitcast.245, f32[4,4,512,128]{3,2,1,0:T(8,128)} %bitcast.244, f32[4,4,512,128]{3,2,1,0:T(8,128)} %bitcast.243, f32[4,4,512,128]{3,2,1,0:T(8,128)} %bitcast.242, f32[4,4,512,128]{3,2,1,0:T(8,128)} %bitcast.241, ...), kind=kLoop, calls=%fused_computation.145 | loop fusion | flops 21233664 | bytes 51904512 | tf_op jit(solution)/shard_map/convert.7
  170.3 2.8 slice_bitcast_fusion.2
  173.1 4.8 %collective-permute-start.4 = (bf16[6,512,128]{2,1,0:T(8,128)(2,1)}, bf16[6,512,128]{2,1,0:T(8,128)(2,1)}, u32[]{:S(2)}, u32[]{:S(2)}) collective-permute-start(bf16[6,512,128]{2,1,0:T(8,128)(2,1)} %get-tuple-element.61), channel_id=1, source_target_pairs={{0,4},{4,8},{8,12},{12,16},{16,20},{20,24},{24,28},{1,5},{5,9},{9,... | collective-permute-start | bytes 2359304 | tf_op jit(solution)/shard_map/ppermute | solution.py:15
  177.9 1.3 collective-permute-start.5
  179.2 2.9 convolution_add_fusion.1
  182.2 1.6 convolution_add_fusion
  184.4 2.4 slice_add_fusion
  187.2 1.3 slice.293
  189.4 1.8 copy.138
  191.3 2.7 reshape_reshape.4
  194.0 6.1 %slice.276 = f32[4,6,512,128]{3,2,1,0:T(8,128)} slice(f32[6,6,512,128]{3,2,1,0:T(8,128)} %get-tuple-element.59), slice={[1:5], [0:6], [0:512], [0:128]} | slice | bytes 12582912 | tf_op jit(solution)/shard_map/slice | solution.py:69
  200.8 1.4 gather_fusion
  202.2 6.6 %all-to-all-start = ((bf16[8,2,64,256]{3,2,1,0:T(8,128)(2,1)}), bf16[8,2,64,256]{3,2,1,0:T(8,128)(2,1)S(1)}, u32[]{:S(2)}, u32[]{:S(2)}) async-start(bf16[8,2,64,256]{3,2,1,0:T(8,128)(2,1)} %bitcast.283), calls=%async_computation | async-start | bytes 1048576 | tf_op jit(solution)/shard_map/all_to_all | solution.py:130
  208.8 2.3 collective-permute-done.4
  211.1 2.9 fusion.2
  214.0 3.2 copy.49
  217.2 1.7 fusion.1
  219.5 2.1 copy-done.3
  222.7 5.9 %collective-permute-start.6 = (bf16[4,512,128]{2,1,0:T(8,128)(2,1)}, bf16[4,512,128]{2,1,0:T(8,128)(2,1)}, u32[]{:S(2)}, u32[]{:S(2)}) collective-permute-start(bf16[4,512,128]{2,1,0:T(8,128)(2,1)} %get-tuple-element.71), channel_id=1, source_target_pairs={{0,1},{1,2},{2,3},{4,5},{5,6},{6,7},{8,9},{9,10},{10,11},{12,13},{... | collective-permute-start | bytes 1572872 | tf_op jit(solution)/shard_map/ppermute | solution.py:15
  228.6 1.7 fusion.85
  231.4 1.3 collective-permute-start.7
  232.7 4.7 %slice.281 = f32[4,4,512,128]{3,2,0,1:T(8,128)} slice(f32[4,6,512,128]{3,2,0,1:T(8,128)} %copy-done.3), slice={[0:4], [1:5], [0:512], [0:128]} | slice | bytes 8388608 | tf_op jit(solution)/shard_map/slice | solution.py:73
  238.5 2.8 fusion.39
  241.3 2.6 copy.51
  244.0 1.3 fusion.38
  245.3 2.0 multiply_convert_fusion
  247.3 123.2 %all-reduce.13.cloned.1.call-done = (f32[27,128,128]{2,1,0:T(8,128)}, f32[1024,256]{1,0:T(8,128)}) async-done(((f32[27,128,128]{2,1,0:T(8,128)}, f32[1024,256]{1,0:T(8,128)}), (f32[27,128,128]{2,1,0:T(8,128)}, f32[1024,256]{1,0:T(8,128)})) %all-reduce.13.cloned.1.call-update) | async-done | bytes 2818064 | tf_op jit(solution)/shard_map/psum | solution.py:181
  370.4 3.0 broadcast_multiply_fusion.1
  (187 shorter events, 47.4 us)
Async XLA Ops:
  7.2 62.2 %copy-start = (bf16[1024,256]{1,0:T(8,128)(2,1)S(1)}, bf16[1024,256]{1,0:T(8,128)(2,1)}, u32[]{:S(2)}) copy-start(bf16[1024,256]{1,0:T(8,128)(2,1)} %param.20) | copy-start | bytes 1572868
  9.7 1.3 copy-start.1
  11.1 7.3 %copy-start.49 = (s32[4,4]{1,0:T(4,128)S(1)}, s32[4,4]{1,0:T(4,128)}, u32[]{:S(2)}) copy-start(s32[4,4]{1,0:T(4,128)} %param.18) | copy-start | bytes 196
  11.1 10.0 %copy-start.46 = (bf16[4,4,64,256]{3,2,1,0:T(8,128)(2,1)S(1)}, bf16[4,4,64,256]{3,2,1,0:T(8,128)(2,1)}, u32[]{:S(2)}) copy-start(bf16[4,4,64,256]{3,2,1,0:T(8,128)(2,1)} %param.21) | copy-start | bytes 1572868
  11.1 19.1 %copy-start.45 = (s32[4,4,9]{2,1,0:T(4,128)S(1)}, s32[4,4,9]{2,1,0:T(4,128)}, u32[]{:S(2)}) copy-start(s32[4,4,9]{2,1,0:T(4,128)} %param.17) | copy-start | bytes 1732
  11.1 19.2 %copy-start.44 = (bf16[27,128,128]{2,1,0:T(8,128)(2,1)S(1)}, bf16[27,128,128]{2,1,0:T(8,128)(2,1)}, u32[]{:S(2)}) copy-start(bf16[27,128,128]{2,1,0:T(8,128)(2,1)} %param.19) | copy-start | bytes 2654212
  12.1 40.6 %collective-permute-start = (bf16[1,4,512,128]{3,2,1,0:T(8,128)(2,1)}, bf16[1,4,512,128]{3,2,1,0:T(8,128)(2,1)S(1)}, u32[]{:S(2)}, u32[]{:S(2)}) collective-permute-start(bf16[1,4,512,128]{3,2,1,0:T(8,128)(2,1)} %get-tuple-element.78), channel_id=1, source_target_pairs={{0,4},{4,8},{8,12},{12,16},{16,20},{20,24},{24,28},{1,5},{5,9},{9,... | collective-permute-start | bytes 1572872 | tf_op jit(solution)/shard_map/ppermute | solution.py:25
  17.0 35.7 %collective-permute-start.1 = (bf16[1,4,512,128]{3,2,1,0:T(8,128)(2,1)}, bf16[1,4,512,128]{3,2,1,0:T(8,128)(2,1)}, u32[]{:S(2)}, u32[]{:S(2)}) collective-permute-start(bf16[1,4,512,128]{3,2,1,0:T(8,128)(2,1)} %get-tuple-element.79), channel_id=1, source_target_pairs={{4,0},{8,4},{12,8},{16,12},{20,16},{24,20},{28,24},{5,1},{9,5},{13... | collective-permute-start | bytes 1572872 | tf_op jit(solution)/shard_map/ppermute | solution.py:26
  22.4 41.8 %all-to-all-start.1 = ((bf16[8,2,64,256]{3,2,1,0:T(8,128)(2,1)}), bf16[8,2,64,256]{3,2,1,0:T(8,128)(2,1)}, u32[]{:S(2)}, u32[]{:S(2)}) async-start(bf16[8,2,64,256]{3,2,1,0:T(8,128)(2,1)} %bitcast.26), calls=%async_computation.1 | async-start | bytes 1048576 | tf_op jit(solution)/shard_map/all_to_all | solution.py:137
  31.7 2.0 copy-start.20
  33.2 8.0 %copy-start.22 = (bf16[2,8,128,128]{3,2,1,0:T(8,128)(2,1)}, bf16[2,8,128,128]{3,2,1,0:T(8,128)(2,1)S(1)}, u32[]{:S(2)}) copy-start(bf16[2,8,128,128]{3,2,1,0:T(8,128)(2,1)S(1)} %copy.83) | copy-start | bytes 1572868
  38.6 3.5 copy-start.24
  41.1 1.8 copy-start.26
  42.1 2.2 copy-start.28
  42.9 2.2 copy-start.39
  43.9 2.1 copy-start.40
  43.9 3.0 copy-start.41
  46.9 5.8 %copy-start.2 = (bf16[4,4,512,128]{3,2,1,0:T(8,128)(2,1)S(1)}, bf16[4,4,512,128]{3,2,1,0:T(8,128)(2,1)}, u32[]{:S(2)}) copy-start(bf16[4,4,512,128]{3,2,1,0:T(8,128)(2,1)} %copy-done.1) | copy-start | bytes 6291460
  52.7 6.3 %copy-start.32 = (bf16[2,8,128,128]{3,2,1,0:T(8,128)(2,1)S(1)}, bf16[2,8,128,128]{3,2,1,0:T(8,128)(2,1)}, u32[]{:S(2)}) copy-start(bf16[2,8,128,128]{3,2,1,0:T(8,128)(2,1)} %copy.89) | copy-start | bytes 1572868
  52.7 7.2 %copy-start.34 = (bf16[2,8,128,128]{3,2,1,0:T(8,128)(2,1)S(1)}, bf16[2,8,128,128]{3,2,1,0:T(8,128)(2,1)}, u32[]{:S(2)}) copy-start(bf16[2,8,128,128]{3,2,1,0:T(8,128)(2,1)} %copy.90) | copy-start | bytes 1572868
  55.1 19.2 %collective-permute-start.2 = (bf16[6,1,512,128]{3,2,1,0:T(8,128)(2,1)}, bf16[6,1,512,128]{3,2,1,0:T(8,128)(2,1)}, u32[]{:S(2)}, u32[]{:S(2)}) collective-permute-start(bf16[6,1,512,128]{3,2,1,0:T(8,128)(2,1)} %get-tuple-element.75), channel_id=1, source_target_pairs={{0,1},{1,2},{2,3},{4,5},{5,6},{6,7},{8,9},{9,10},{10,11},{12,13},{... | collective-permute-start | bytes 2359304 | tf_op jit(solution)/shard_map/ppermute | solution.py:25
  57.3 17.1 %collective-permute-start.3 = (bf16[6,1,512,128]{3,2,1,0:T(8,128)(2,1)}, bf16[6,1,512,128]{3,2,1,0:T(8,128)(2,1)}, u32[]{:S(2)}, u32[]{:S(2)}) collective-permute-start(bf16[6,1,512,128]{3,2,1,0:T(8,128)(2,1)} %get-tuple-element.74), channel_id=1, source_target_pairs={{1,0},{2,1},{3,2},{5,4},{6,5},{7,6},{9,8},{10,9},{11,10},{13,12},{... | collective-permute-start | bytes 2359304 | tf_op jit(solution)/shard_map/ppermute | solution.py:26
  78.9 3.7 copy-start.8
  78.9 4.2 %copy-start.10 = (bf16[4,4,512,128]{3,2,1,0:T(8,128)(2,1)}, bf16[4,4,512,128]{3,2,1,0:T(8,128)(2,1)S(1)}, u32[]{:S(2)}) copy-start(bf16[4,4,512,128]{3,2,1,0:T(8,128)(2,1)S(1)} %get-tuple-element.95) | copy-start | bytes 6291460
  78.9 7.9 %copy-start.6 = (bf16[4,4,512,128]{3,2,1,0:T(8,128)(2,1)}, bf16[4,4,512,128]{3,2,1,0:T(8,128)(2,1)S(1)}, u32[]{:S(2)}) copy-start(bf16[4,4,512,128]{3,2,1,0:T(8,128)(2,1)S(1)} %get-tuple-element.64) | copy-start | bytes 6291460
  78.9 3.2 copy-start.5
  84.7 1.6 copy-start.4
  87.4 6.5 %copy-start.48 = (bf16[16,512,1152]{2,1,0:T(8,128)(2,1)}, bf16[16,512,1152]{2,1,0:T(8,128)(2,1)S(1)}, u32[]{:S(2)}) copy-start(bf16[16,512,1152]{2,1,0:T(8,128)(2,1)S(1)} %constant_dynamic-update-slice_fusion) | copy-start | bytes 56623108
  109.0 1.7 copy-start.9
  110.8 1.8 copy-start.7
  116.3 1.0 copy-start.21
  117.3 1.0 copy-start.23
  118.4 1.0 copy-start.25
  119.4 1.0 copy-start.27
  120.5 2.7 copy-start.29
  123.2 2.7 copy-start.30
  125.9 2.8 copy-start.31
  128.6 2.7 copy-start.33
  131.3 3.1 copy-start.35
  151.4 5.8 %copy-start.11 = (f32[16,512,128]{2,1,0:T(8,128)S(1)}, f32[16,512,128]{2,1,0:T(8,128)}, u32[]{:S(2)}) copy-start(f32[16,512,128]{2,1,0:T(8,128)} %fusion.70) | copy-start | bytes 12582916
  170.3 8.9 %copy-start.13 = (f32[28,16384]{1,0:T(8,128)S(1)}, f32[28,16384]{1,0:T(8,128)}, u32[]{:S(2)}) copy-start(f32[28,16384]{1,0:T(8,128)} %fusion.34) | copy-start | bytes 5505028
  170.3 11.8 %copy-start.36 = (f32[16,128,128]{2,1,0:T(8,128)S(1)}, f32[16,128,128]{2,1,0:T(8,128)}, u32[]{:S(2)}) copy-start(f32[16,128,128]{2,1,0:T(8,128)} %fusion.78) | copy-start | bytes 3145732
  173.1 38.0 %collective-permute-start.4 = (bf16[6,512,128]{2,1,0:T(8,128)(2,1)}, bf16[6,512,128]{2,1,0:T(8,128)(2,1)}, u32[]{:S(2)}, u32[]{:S(2)}) collective-permute-start(bf16[6,512,128]{2,1,0:T(8,128)(2,1)} %get-tuple-element.61), channel_id=1, source_target_pairs={{0,4},{4,8},{8,12},{12,16},{16,20},{20,24},{24,28},{1,5},{5,9},{9,... | collective-permute-start | bytes 2359304 | tf_op jit(solution)/shard_map/ppermute | solution.py:15
  177.9 39.3 %collective-permute-start.5 = (bf16[6,512,128]{2,1,0:T(8,128)(2,1)}, bf16[6,512,128]{2,1,0:T(8,128)(2,1)}, u32[]{:S(2)}, u32[]{:S(2)}) collective-permute-start(bf16[6,512,128]{2,1,0:T(8,128)(2,1)} %get-tuple-element.60), channel_id=1, source_target_pairs={{4,0},{8,4},{12,8},{16,12},{20,16},{24,20},{28,24},{5,1},{9,5},{13... | collective-permute-start | bytes 2359304 | tf_op jit(solution)/shard_map/ppermute | solution.py:15
  179.2 4.6 %copy-start.16 = (f32[28,16384]{1,0:T(8,128)S(1)}, f32[28,16384]{1,0:T(8,128)}, u32[]{:S(2)}) copy-start(f32[28,16384]{1,0:T(8,128)} %fusion.21) | copy-start | bytes 5505028
  179.2 4.6 %copy-start.17 = (f32[28,16384]{1,0:T(8,128)S(1)}, f32[28,16384]{1,0:T(8,128)}, u32[]{:S(2)}) copy-start(f32[28,16384]{1,0:T(8,128)} %fusion.27) | copy-start | bytes 5505028
  179.2 4.6 %copy-start.18 = (f32[28,16384]{1,0:T(8,128)S(1)}, f32[28,16384]{1,0:T(8,128)}, u32[]{:S(2)}) copy-start(f32[28,16384]{1,0:T(8,128)} %fusion.15) | copy-start | bytes 5505028
  182.2 1.7 copy-start.14
  182.2 2.3 copy-start.15
  187.2 2.2 copy-start.37
  194.0 6.1 %copy-start.38 = (bf16[1024,1024]{1,0:T(8,128)(2,1)S(1)}, bf16[1024,1024]{1,0:T(8,128)(2,1)}, u32[]{:S(2)}) copy-start(bf16[1024,1024]{1,0:T(8,128)(2,1)} %reshape_reshape.4) | copy-start | bytes 6291460
  202.2 35.2 %all-to-all-start = ((bf16[8,2,64,256]{3,2,1,0:T(8,128)(2,1)}), bf16[8,2,64,256]{3,2,1,0:T(8,128)(2,1)S(1)}, u32[]{:S(2)}, u32[]{:S(2)}) async-start(bf16[8,2,64,256]{3,2,1,0:T(8,128)(2,1)} %bitcast.283), calls=%async_computation | async-start | bytes 1048576 | tf_op jit(solution)/shard_map/all_to_all | solution.py:130
  208.8 161.6 %all-reduce.13.cloned.1.call-start = ((), (), s32[]{:S(2)}) async-start(), calls=%async_computation.2 | async-start | bytes 5636096 | tf_op jit(solution)/shard_map/psum | solution.py:181
  218.9 2.7 copy-start.3
  221.6 7.0 %copy-start.19 = (bf16[16,64,256]{2,1,0:T(8,128)(2,1)S(1)}, bf16[16,64,256]{2,1,0:T(8,128)(2,1)}, u32[]{:S(2)}) copy-start(bf16[16,64,256]{2,1,0:T(8,128)(2,1)} %scatter_fusion.1) | copy-start | bytes 1572868
  222.7 15.8 %collective-permute-start.6 = (bf16[4,512,128]{2,1,0:T(8,128)(2,1)}, bf16[4,512,128]{2,1,0:T(8,128)(2,1)}, u32[]{:S(2)}, u32[]{:S(2)}) collective-permute-start(bf16[4,512,128]{2,1,0:T(8,128)(2,1)} %get-tuple-element.71), channel_id=1, source_target_pairs={{0,1},{1,2},{2,3},{4,5},{5,6},{6,7},{8,9},{9,10},{10,11},{12,13},{... | collective-permute-start | bytes 1572872 | tf_op jit(solution)/shard_map/ppermute | solution.py:15
  230.3 1.0 copy-start.47
  231.4 12.6 %collective-permute-start.7 = (bf16[4,512,128]{2,1,0:T(8,128)(2,1)S(1)}, bf16[4,512,128]{2,1,0:T(8,128)(2,1)S(1)}, u32[]{:S(2)}, u32[]{:S(2)}) collective-permute-start(bf16[4,512,128]{2,1,0:T(8,128)(2,1)S(1)} %copy-done.47), channel_id=1, source_target_pairs={{1,0},{2,1},{3,2},{5,4},{6,5},{7,6},{9,8},{10,9},{11,10},{13,12},{... | collective-permute-start | bytes 1572872 | tf_op jit(solution)/shard_map/ppermute | solution.py:15
  238.5 5.5 %copy-start.42 = (bf16[16,64,256]{2,1,0:T(8,128)(2,1)}, bf16[16,64,256]{2,1,0:T(8,128)(2,1)S(1)}, u32[]{:S(2)}) copy-start(bf16[16,64,256]{2,1,0:T(8,128)(2,1)S(1)} %scatter_fusion) | copy-start | bytes 1572868
  241.3 4.0 %copy-start.12 = (f32[16,4,2,4,2,4,2,128]{7,6,5,4,3,2,1,0:T(2,128)S(1)}, f32[16,4,2,4,2,4,2,128]{7,6,5,4,3,2,1,0:T(2,128)}, u32[]{:S(2)}) copy-start(f32[16,4,2,4,2,4,2,128]{7,6,5,4,3,2,1,0:T(2,128)} %copy.46) | copy-start | bytes 12582916
  370.4 3.0 copy-start.43
Sparse Core Ops, SparseCore 0:
  230.5 139.8 all-reduce.12
where the time goes:
time: 388 us; the launch traced here: 381 us
  waiting for transfers between devices  125 us (32%)
  local copies, waits for them, and re-layouts  82.9 us (21%)
  matrix products  75 us (19%)
  other arithmetic  45 us (12%)
  starting transfers between devices  37.7 us (10%)
  between operations  15.4 us (4%)
    psum x1, waiting for transfers between devices, local(): lax.psum((sub_grad[:27].reshape(27, channels, channels), down_grad), ('gx...  123 us
    unnamed x137, local copies, waits for them, and re-layouts  39.3 us
    dot_general x9, matrix products, local(): lax.dot_general(selector, outer.reshape(bricks, channels * channels), (((...  24.7 us
    dot_general x9, matrix products, local(): jnp.einsum('bvd,bcd->bvc', pre_grad, chosen[direction], preferred_element...  18.3 us
    another operation x2, other arithmetic  13.7 us
    ppermute x4, starting transfers between devices, from_behind(): lax.ppermute(value, axis, [(source, source + steps) for source in range(l...  13.3 us
    dot_general x1, matrix products, local(): jnp.einsum('nho,nor->nhr', joined_windows(extended), stacked_weights, pre...  12.8 us
    dot_general x9, matrix products, local(): jnp.einsum('bvc,bvd->bcd', window(extended, stepping_x, stepping_y), pre_...  10.4 us
  transfers between devices with their start and end apart: 11, of which 2 were waited for; matrix products, arithmetic and copies ran while one was open for 24% of the time, Pallas kernels for 0%

commit v1 on v0

v1 whole, which is shorter than its diff:
```python
import functools

import jax
import jax.numpy as jnp
from jax import lax
from jax.experimental import pallas as pl
from jax.experimental.pallas import tpu as pltpu
from jax.sharding import PartitionSpec as P

MESH = pl.DeviceIdType.MESH
E = 8
NEIGHBOURS = [(-1, -1), (-1, 0), (-1, 1), (0, -1), (0, 0), (0, 1), (1, -1), (1, 0), (1, 1)]
HALO = [k for k in range(9) if k != 4]
F32 = jnp.float32
BF16 = jnp.bfloat16
VMEM_LIMIT = 52 * 1024 * 1024


def position():
    return lax.axis_index("gx"), lax.axis_index("gy")


def exists(nx, ny, gx, gy, k):
    dx, dy = NEIGHBOURS[k]
    x, y = gx + dx, gy + dy
    return (x >= 0) & (x < nx) & (y >= 0) & (y < ny)


def edge(ref, width_x, width_y, k):
    dx, dy = NEIGHBOURS[k]
    sx = {-1: 0, 0: slice(None), 1: width_x - 1}[dx]
    sy = {-1: 0, 0: slice(None), 1: width_y - 1}[dy]
    return ref.at[sx, sy]


def slot(halo, k):
    hx, hy, hc = halo
    dx, dy = NEIGHBOURS[k]
    if dy == 0:
        return hx.at[(dx + 1) // 2]
    if dx == 0:
        return hy.at[(dy + 1) // 2]
    return hc.at[(dx + 1) // 2 * 2 + (dy + 1) // 2]


def halo_copy(nx, ny, gx, gy, source, halo, send, recv, k):
    dx, dy = NEIGHBOURS[k]
    return pltpu.make_async_remote_copy(
        src_ref=edge(source, source.shape[0], source.shape[1], k),
        dst_ref=slot(halo, 8 - k),
        send_sem=send.at[k],
        recv_sem=recv.at[8 - k],
        device_id=(gx + dx, gy + dy),
        device_id_type=MESH,
    )


def halo_arrival(nx, ny, gx, gy, source, halo, send, recv, k):
    dx, dy = NEIGHBOURS[k]
    return pltpu.make_async_remote_copy(
        src_ref=edge(source, source.shape[0], source.shape[1], 8 - k),
        dst_ref=slot(halo, k),
        send_sem=send.at[8 - k],
        recv_sem=recv.at[k],
        device_id=(gx + dx, gy + dy),
        device_id_type=MESH,
    )


def halo_fill(source, halo, recv, k):
    return pltpu.make_async_copy(
        edge(source, source.shape[0], source.shape[1], k), slot(halo, k), recv.at[k]
    )


def start_halo(nx, ny, gx, gy, source, halo, send, recv):
    for k in HALO:
        there = exists(nx, ny, gx, gy, k)

        @pl.when(there)
        def _(k=k):
            halo_copy(nx, ny, gx, gy, source, halo, send, recv, k).start()

        @pl.when(jnp.logical_not(there))
        def _(k=k):
            halo_fill(source, halo, recv, k).start()


def finish_halo(nx, ny, gx, gy, source, halo, send, recv):
    for k in HALO:
        there = exists(nx, ny, gx, gy, k)

        @pl.when(there)
        def _(k=k):
            halo_copy(nx, ny, gx, gy, source, halo, send, recv, k).wait_send()
            halo_arrival(nx, ny, gx, gy, source, halo, send, recv, k).wait_recv()

        @pl.when(jnp.logical_not(there))
        def _(k=k):
            halo_fill(source, halo, recv, k).wait()


def exchange_copy(nx, gx, gy, outgoing, incoming, send, recv, shift):
    peer = lax.rem(gx + shift, nx)
    return pltpu.make_async_remote_copy(
        src_ref=outgoing.at[peer],
        dst_ref=incoming.at[gx],
        send_sem=send.at[shift],
        recv_sem=recv.at[shift],
        device_id=(peer, gy),
        device_id_type=MESH,
    )


def exchange_arrival(nx, gx, gy, outgoing, incoming, send, recv, shift):
    peer = lax.rem(gx + nx - shift, nx)
    return pltpu.make_async_remote_copy(
        src_ref=outgoing.at[peer],
        dst_ref=incoming.at[peer],
        send_sem=send.at[shift],
        recv_sem=recv.at[shift],
        device_id=(peer, gy),
        device_id_type=MESH,
    )


def start_exchange(nx, gx, gy, outgoing, incoming, send, recv):
    pltpu.make_async_copy(outgoing.at[gx], incoming.at[gx], recv.at[0]).start()
    for shift in range(1, nx):
        exchange_copy(nx, gx, gy, outgoing, incoming, send, recv, shift).start()


def finish_exchange(nx, gx, gy, outgoing, incoming, send, recv):
    pltpu.make_async_copy(outgoing.at[gx], incoming.at[gx], recv.at[0]).wait()
    for shift in range(1, nx):
        exchange_copy(nx, gx, gy, outgoing, incoming, send, recv, shift).wait_send()
        exchange_arrival(nx, gx, gy, outgoing, incoming, send, recv, shift).wait_recv()


def greet(nx, ny, gx, gy, partners):
    barrier = pltpu.get_barrier_semaphore()
    for k in HALO:
        dx, dy = NEIGHBOURS[k]

        @pl.when(exists(nx, ny, gx, gy, k))
        def _(dx=dx, dy=dy):
            pl.semaphore_signal(
                barrier, inc=1, device_id=(gx + dx, gy + dy), device_id_type=MESH
            )

    for shift in range(1, nx):
        pl.semaphore_signal(
            barrier, inc=1, device_id=(lax.rem(gx + shift, nx), gy), device_id_type=MESH
        )
    for partner in partners:
        pl.semaphore_signal(barrier, inc=1, device_id=partner, device_id_type=MESH)
    count = nx - 1 + len(partners)
    for k in HALO:
        count = count + jnp.where(exists(nx, ny, gx, gy, k), 1, 0)
    pl.semaphore_wait(barrier, count)


def open_kernel(nx, ny, order, features, cotangent, hx, hy, hc, incoming, outgoing, hs, hr, es, er):
    gx, gy = position()
    halo = (hx, hy, hc)
    greet(nx, ny, gx, gy, [])
    start_halo(nx, ny, gx, gy, features, halo, hs, hr)
    share = outgoing.shape[1]
    for peer in range(nx):
        for i in range(share):
            outgoing[peer, i] = cotangent[order[peer * share + i]]
    start_exchange(nx, gx, gy, outgoing, incoming, es, er)
    finish_exchange(nx, gx, gy, outgoing, incoming, es, er)
    finish_halo(nx, ny, gx, gy, features, halo, hs, hr)


def groups(nx, ny):
    deep = 4 if nx % 4 == 0 else 1
    return [
        (axis, stride, size)
        for axis, stride, size in (
            (1, 1, 2),
            (1, 2, ny // 2),
            (0, 1, nx // deep),
            (0, nx // deep, deep),
        )
        if size > 1
    ]


def member(gx, gy, group, shift):
    axis, stride, size = group
    here = (gx, gy)[axis]
    own = lax.rem(lax.div(here, stride), size)
    other = lax.rem(own + shift, size)
    there = here + (other - own) * stride
    return own, other, ((there, gy) if axis == 0 else (gx, there))


def reduce_all(nx, ny, gx, gy, partial, total, sends, recvs, ss, rs, gs, gr):
    rows = partial.shape[0]
    plan = groups(nx, ny)
    base, length = 0, rows
    bases = []
    sem = 0
    for stage, group in enumerate(plan):
        size = group[2]
        chunk = length // size
        copies = []
        own = None
        for shift in range(1, size):
            own, other, device = member(gx, gy, group, shift)
            start = pl.multiple_of(base + other * chunk, 16)
            sends[stage][shift - 1] = partial[pl.ds(start, chunk)].astype(BF16)
            copy = pltpu.make_async_remote_copy(
                src_ref=sends[stage].at[shift - 1],
                dst_ref=recvs[stage].at[shift - 1],
                send_sem=ss.at[sem],
                recv_sem=rs.at[sem],
                device_id=device,
                device_id_type=MESH,
            )
            copy.start()
            copies.append(copy)
            sem += 1
        bases.append(base)
        base = pl.multiple_of(base + own * chunk, 16)
        length = chunk
        for copy in copies:
            copy.wait()
        value = partial[pl.ds(base, chunk)]
        for shift in range(1, size):
            value = value + recvs[stage][shift - 1].astype(F32)
        partial[pl.ds(base, chunk)] = value
    total[pl.ds(base, length)] = (partial[pl.ds(base, length)]).astype(BF16)
    sem = 0
    for stage in reversed(range(len(plan))):
        group = plan[stage]
        size = group[2]
        copies = []
        for shift in range(1, size):
            own, other, device = member(gx, gy, group, shift)
            back = lax.rem(own + size - shift, size)
            copies.append(
                (
                    pltpu.make_async_remote_copy(
                        src_ref=total.at[pl.ds(base, length)],
                        dst_ref=total.at[pl.ds(base, length)],
                        send_sem=gs.at[sem],
                        recv_sem=gr.at[sem],
                        device_id=device,
                        device_id_type=MESH,
                    ),
                    pl.multiple_of(bases[stage] + back * length, 16),
                    sem,
                    device,
                )
            )
            copies[-1][0].start()
            sem += 1
        for copy, start, index, device in copies:
            copy.wait_send()
            pltpu.make_async_remote_copy(
                src_ref=total.at[pl.ds(base, length)],
                dst_ref=total.at[pl.ds(start, length)],
                send_sem=gs.at[index],
                recv_sem=gr.at[index],
                device_id=device,
                device_id_type=MESH,
            ).wait_recv()
        base = bases[stage]
        length = length * size


def close_kernel(
    nx, ny, stages, pre_grad, outgoing, partial_in, hx, hy, hc, incoming, result, *scratch
):
    sends, recvs = scratch[:stages], scratch[stages : 2 * stages]
    partial, total, hs, hr, es, er, ss, rs, gs, gr, ls = scratch[2 * stages :]
    gx, gy = position()
    halo = (hx, hy, hc)
    load = pltpu.make_async_copy(partial_in, partial, ls)
    load.start()
    plan = groups(nx, ny)
    partners = [
        member(gx, gy, group, shift)[2] for group in plan for shift in range(1, group[2])
    ]
    greet(nx, ny, gx, gy, partners)
    start_halo(nx, ny, gx, gy, pre_grad, halo, hs, hr)
    start_exchange(nx, gx, gy, outgoing, incoming, es, er)
    load.wait()
    reduce_all(nx, ny, gx, gy, partial, total, sends, recvs, ss, rs, gs, gr)
    result[...] = total[...]
    finish_exchange(nx, gx, gy, outgoing, incoming, es, er)
    finish_halo(nx, ny, gx, gy, pre_grad, halo, hs, hr)


def ext_source(width_x, width_y, refs, x, y):
    own, hx, hy, hc = refs
    sx = 0 if x < 0 else (2 if x >= width_x else 1)
    sy = 0 if y < 0 else (2 if y >= width_y else 1)
    if sx == 1 and sy == 1:
        return own, (x, y)
    if sy == 1:
        return hx, (sx // 2, y)
    if sx == 1:
        return hy, (sy // 2, x)
    return hc, (sx // 2 * 2 + sy // 2,)


def voxel_order(transposed):
    row = lax.broadcasted_iota(jnp.int32, (E**3, E**3), 1 if transposed else 0)
    column = lax.broadcasted_iota(jnp.int32, (E**3, E**3), 0 if transposed else 1)
    sub, cell = row // 64, row % 64
    a = (cell // 16) * 2 + sub // 4
    b = (cell // 4) % 4 * 2 + (sub // 2) % 2
    c = cell % 4 * 2 + sub % 2
    return jnp.where(column == (a * 8 + b) * 8 + c, 1.0, 0.0).astype(BF16)


def dot(a, b, dims):
    return lax.dot_general(a, b, (dims, ((), ())), preferred_element_type=F32)


def forward_kernel(
    width_x,
    width_y,
    occupancy,
    offsets,
    rank,
    features,
    hx,
    hy,
    hc,
    received,
    w_sub,
    w_down,
    pre_grad,
    moved,
    partial,
    returned,
    ext,
    ext_t,
    weights,
    preact,
    patches,
    hidden_grad,
    acc,
):
    bricks = width_x * width_y
    wide = width_y + 2
    order = voxel_order(False)
    cells = [(x, y) for x in range(-1, width_x + 1) for y in range(-1, width_y + 1)]
    refs = (features, hx, hy, hc)
    for first in range(0, len(cells), 2):
        pair = []
        for x, y in cells[first : first + 2]:
            ref, at = ext_source(width_x, width_y, refs, x, y)
            pair.append(ref[at])
        moved_pair = dot(order, jnp.concatenate(pair, 1), ((1,), (0,))).astype(BF16)
        for j in range(2):
            column = moved_pair[:, j * 128 : (j + 1) * 128]
            ext[first + j] = column
            ext_t[first + j] = column.T
    for p in range(bricks):
        returned[pl.ds(p * 64, 64)] = received[rank[p]]
    acc[...] = jnp.zeros_like(acc)

    def spread(g, _):
        rows = pl.ds(pl.multiple_of(g * 256, 256), 256)
        hidden_grad[rows] = dot(returned[rows], w_down[...], ((1,), (1,)))
        return 0

    lax.fori_loop(0, bricks // 4, spread, 0)

    def brick(p, _):
        x, y = p // width_y, p % width_y
        rows = pl.ds(pl.multiple_of(p * 64, 64), 64)
        present = occupancy[p].astype(F32)
        at = [(x + 1 + dx) * wide + y + 1 + dy for dx, dy in NEIGHBOURS]
        codes = [offsets[p * 9 + k] for k in range(9)]
        for k in range(9):
            chosen = w_sub[jnp.minimum(codes[k], 26)]
            weights[pl.ds(k * 128, 128)] = jnp.where(codes[k] < 27, chosen, jnp.zeros_like(chosen))
        window = jnp.concatenate([ext[i] for i in at], 1)
        preact[...] = dot(window, weights[...], ((1,), (0,)))
        for s in range(8):
            part = pl.ds(s * 64, 64)
            lanes = pl.ds(s * 128, 128)
            pre = preact[part]
            sig = jax.nn.sigmoid(pre)
            own = ext[at[4], part].astype(F32)
            patches[rows, lanes] = (present * (own + pre * sig)).astype(BF16)
            slope = sig * (1.0 + pre * (1.0 - sig))
            pre_grad[p, part] = (present * hidden_grad[rows, lanes] * slope).astype(BF16)
        window_t = jnp.concatenate([ext_t[i] for i in at], 0)
        outer = dot(window_t, pre_grad[p], ((1,), (0,)))
        for k in range(9):
            acc[codes[k]] += outer[k * 128 : (k + 1) * 128]
        return 0

    lax.fori_loop(0, bricks, brick, 0)
    shifted = dot(patches[...], w_down[...], ((1,), (0,))).astype(BF16)
    for p in range(bricks):
        moved[rank[p]] = shifted[p * 64 : (p + 1) * 64]
    for o in range(27):
        partial[pl.ds(o * 128, 128)] = acc[o]
    top = 27 * 128
    for s in range(8):
        grad = dot(patches[:, s * 128 : (s + 1) * 128], returned[...], ((0,), (0,)))
        for half in range(2):
            partial[pl.ds(top + half * 1024 + s * 128, 128)] = grad[:, half * 128 : half * 128 + 128]
    top += 2048
    if partial.shape[0] > top:
        partial[pl.ds(top, partial.shape[0] - top)] = jnp.zeros(
            (partial.shape[0] - top, 128), F32
        )


def backward_kernel(
    width_x,
    width_y,
    devices,
    occupancy,
    offsets,
    rank,
    pre_grad,
    hx,
    hy,
    hc,
    returned,
    received,
    total,
    w_sub,
    w_down,
    coarse,
    feature_grad,
    sub_grad,
    down_grad,
    ext,
    weights,
    hidden_grad,
):
    bricks = width_x * width_y
    wide = width_y + 2
    refs = (pre_grad, hx, hy, hc)
    cells = [(x, y) for x in range(-1, width_x + 1) for y in range(-1, width_y + 1)]
    for i, (x, y) in enumerate(cells):
        ref, at = ext_source(width_x, width_y, refs, x, y)
        ext[i] = ref[at]
    for p in range(bricks):
        coarse[p // width_y, p % width_y] = received[rank[p]]
    scale = 1.0 / devices
    for o in range(27):
        sub_grad[o] = total[pl.ds(o * 128, 128)].astype(F32) * scale
    for half in range(2):
        down_grad[:, pl.ds(half * 128, 128)] = (
            total[pl.ds(27 * 128 + half * 1024, 1024)].astype(F32) * scale
        )

    def spread(g, _):
        rows = pl.ds(pl.multiple_of(g * 256, 256), 256)
        hidden_grad[rows] = dot(returned[rows], w_down[...], ((1,), (1,)))
        return 0

    lax.fori_loop(0, bricks // 4, spread, 0)
    back = voxel_order(True)

    def column(p, _):
        x, y = p // width_y, p % width_y
        at = [(x + 1 + dx) * wide + y + 1 + dy for dx, dy in NEIGHBOURS]
        for k in range(9):
            code = offsets[p * 9 + k]
            chosen = w_sub[jnp.maximum(26 - code, 0)]
            weights[:, k * 128 : (k + 1) * 128] = jnp.where(
                code < 27, chosen, jnp.zeros_like(chosen)
            )
        window = jnp.concatenate([ext[i] for i in at], 1)
        conv = dot(window, weights[...], ((1,), (1,)))
        rows = pl.ds(pl.multiple_of(p * 64, 64), 64)
        spread_rows = jnp.concatenate(
            [hidden_grad[rows, s * 128 : (s + 1) * 128] for s in range(8)], 0
        )
        return (occupancy[p].astype(F32) * (spread_rows + conv)).astype(BF16)

    def pair(i, _):
        p = i * 2
        both = jnp.concatenate([column(p, 0), column(p + 1, 0)], 1)
        out = dot(back, both, ((1,), (0,))).astype(BF16)
        feature_grad[p // width_y, p % width_y] = out[:, :128]
        feature_grad[(p + 1) // width_y, (p + 1) % width_y] = out[:, 128:]
        return 0

    lax.fori_loop(0, bricks // 2, pair, 0)


def ranks(keys):
    rank = jnp.sum((keys[None, :] < keys[:, None]).astype(jnp.int32), 1)
    places = jnp.arange(keys.shape[0], dtype=jnp.int32)
    order = jnp.sum((rank[None, :] == places[:, None]).astype(jnp.int32) * places[None, :], 1)
    return rank, order


def local(nx, ny, features, occupancy, pair_offset, owner, w_sub, w_down, cotangent):
    width_x, width_y, voxels, channels = features.shape
    bricks = width_x * width_y
    cells, out_channels = cotangent.shape[2:]
    share = bricks // nx
    occupied = occupancy.reshape(bricks)
    offsets = pair_offset.reshape(bricks * 9)
    targets = owner.reshape(bricks)
    places = jnp.arange(bricks, dtype=jnp.int32)
    source = (2 * lax.axis_index("gx") - targets + nx) % nx
    send_rank, _ = ranks(targets * bricks + places)
    cell_rank, cell_order = ranks(source * bricks + places)

    any_spec = pl.BlockSpec(memory_space=pl.ANY)
    vmem = pl.BlockSpec(memory_space=pltpu.VMEM)
    smem = pl.BlockSpec(memory_space=pltpu.SMEM)
    shape = jax.ShapeDtypeStruct
    halo_shapes = [
        shape((2, width_y, voxels, channels), BF16),
        shape((2, width_x, voxels, channels), BF16),
        shape((4, voxels, channels), BF16),
    ]
    block = shape((nx, share, cells, out_channels), BF16)
    dma = pltpu.SemaphoreType.DMA

    hx, hy, hc, received = pl.pallas_call(
        functools.partial(open_kernel, nx, ny),
        out_shape=halo_shapes + [block],
        in_specs=[smem, any_spec, vmem],
        out_specs=[any_spec] * 4,
        scratch_shapes=[
            pltpu.VMEM(block.shape, BF16),
            dma((9,)),
            dma((9,)),
            dma((nx,)),
            dma((nx,)),
        ],
        compiler_params=pltpu.CompilerParams(
            collective_id=0, has_side_effects=True, vmem_limit_bytes=VMEM_LIMIT
        ),
        name="open_exchange",
    )(cell_order, features, cotangent.reshape(bricks, cells, out_channels))

    unit = 16 * nx * ny
    rows = -(-(27 * channels + 2048) // unit) * unit
    brick_shape = (bricks, voxels, channels)
    pre_grad, moved, partial, returned = pl.pallas_call(
        functools.partial(forward_kernel, width_x, width_y),
        out_shape=[
            shape(brick_shape, BF16),
            shape((bricks, cells, out_channels), BF16),
            shape((rows, 128), F32),
            shape((bricks * cells, out_channels), BF16),
        ],
        in_specs=[smem] * 3 + [vmem] * 7,
        out_specs=[vmem] * 4,
        scratch_shapes=[
            pltpu.VMEM(((width_x + 2) * (width_y + 2), voxels, channels), BF16),
            pltpu.VMEM(((width_x + 2) * (width_y + 2), channels, voxels), BF16),
            pltpu.VMEM((9 * channels, channels), BF16),
            pltpu.VMEM((voxels, channels), F32),
            pltpu.VMEM((bricks * cells, 8 * channels), BF16),
            pltpu.VMEM((bricks * cells, 8 * channels), F32),
            pltpu.VMEM((28, channels, channels), F32),
        ],
        compiler_params=pltpu.CompilerParams(vmem_limit_bytes=VMEM_LIMIT),
        name="forward",
    )(
        occupied,
        offsets,
        send_rank,
        features,
        hx,
        hy,
        hc,
        received.reshape(bricks, cells, out_channels),
        w_sub,
        w_down,
    )

    plan = groups(nx, ny)
    buffers = []
    length = rows
    count = 0
    for _, _, size in plan:
        length //= size
        buffers.append(pltpu.VMEM((size - 1, length, 128), BF16))
        count += size - 1
    gx_halo, gy_halo, gc_halo, arrived, total = pl.pallas_call(
        functools.partial(close_kernel, nx, ny, len(plan)),
        out_shape=halo_shapes + [block, shape((rows, 128), BF16)],
        in_specs=[any_spec] * 3,
        out_specs=[any_spec] * 4 + [vmem],
        scratch_shapes=buffers
        + buffers
        + [
            pltpu.VMEM((rows, 128), F32),
            pltpu.VMEM((rows, 128), BF16),
            dma((9,)),
            dma((9,)),
            dma((nx,)),
            dma((nx,)),
            dma((count,)),
            dma((count,)),
            dma((count,)),
            dma((count,)),
            dma(()),
        ],
        compiler_params=pltpu.CompilerParams(
            collective_id=1, has_side_effects=True, vmem_limit_bytes=VMEM_LIMIT
        ),
        name="close_exchange",
    )(pre_grad.reshape(features.shape), moved.reshape(block.shape), partial)

    return pl.pallas_call(
        functools.partial(backward_kernel, width_x, width_y, nx * ny),
        out_shape=[
            shape(cotangent.shape, BF16),
            shape(features.shape, BF16),
            shape(w_sub.shape, F32),
            shape(w_down.shape, F32),
        ],
        in_specs=[smem] * 3 + [vmem] * 9,
        out_specs=[vmem] * 4,
        scratch_shapes=[
            pltpu.VMEM(((width_x + 2) * (width_y + 2), voxels, channels), BF16),
            pltpu.VMEM((channels, 9 * channels), BF16),
            pltpu.VMEM((bricks * cells, 8 * channels), F32),
        ],
        compiler_params=pltpu.CompilerParams(vmem_limit_bytes=VMEM_LIMIT),
        name="backward",
    )(
        occupied,
        offsets,
        cell_rank,
        pre_grad.reshape(features.shape),
        gx_halo,
        gy_halo,
        gc_halo,
        returned,
        arrived.reshape(bricks, cells, out_channels),
        total,
        w_sub,
        w_down,
    )


def solution(mesh):
    in_specs = (
        P("gx", "gy", None, None),
        P("gx", "gy"),
        P("gx", "gy", None),
        P("gx", "gy"),
        P(),
        P(),
        P("gx", "gy", None, None),
    )
    out_specs = (P("gx", "gy", None, None), P("gx", "gy", None, None), P(), P())
    return jax.shard_map(
        functools.partial(local, mesh.shape["gx"], mesh.shape["gy"]),
        mesh=mesh,
        in_specs=in_specs,
        out_specs=out_specs,
        check_vma=False,
    )
```

time: 388 us -> 171 us (0.44); the launches traced: 381 us -> 171 us
  Pallas kernels: 0 us -> 166 us
  waiting for transfers between devices: 125 us -> 0 us
  local copies, waits for them, and re-layouts: 82.9 us -> 3.55 us
  matrix products: 75 us -> 0 us
  other arithmetic: 45 us -> 1.19 us
  starting transfers between devices: 37.7 us -> 0 us
  between operations: 15.4 us -> 0.68 us
    pallas_call x0 -> x4, Pallas kernels: none -> 166 us  [the longest x1 71.5 us: local(): pl.pallas_call(functools.partial(close_kernel, nx, ny, len(plan)), out_sh...]
    psum x1 -> x0, waiting for transfers between devices: 123 us -> none  [local(): lax.psum((sub_grad[:27].reshape(27, channels, channels), down_grad), ('gx...]
    dot_general x40 -> x0, matrix products: 75 us -> none  [the longest x9 24.7 us: local(): lax.dot_general(selector, outer.reshape(bricks, channels * channels), (((...]
    unnamed x137 -> x4, local copies, waits for them, and re-layouts: 39.3 us -> 1.83 us
    ppermute x8 -> x0, starting transfers between devices: 23.4 us -> none  [the longest x4 13.3 us: from_behind(): lax.ppermute(value, axis, [(source, source + steps) for source in range(l...]
    all_to_all x2 -> x0, starting transfers between devices: 14.3 us -> none  [the longest x1 7.69 us: local(): lax.all_to_all(returning, 'gx', split_axis=0, concat_axis=0, tiled=True)]
    another operation x2 -> x0, other arithmetic: 13.7 us -> none
    slice x5 -> x0, local copies, waits for them, and re-layouts: 13.2 us -> none  [the longest x1 6.12 us: fold_rims(): inner_rows = spread[1:-1]]
  transfers between devices with their start and end apart: 11 -> 0, of which waited for: 2 -> 0; matrix products, arithmetic and copies ran while one was open for 24% -> 0% of each run, Pallas kernels for 0% -> 0%
where the time goes in v1:
time: 171 us
  Pallas kernels  166 us (97%)
  local copies, waits for them, and re-layouts  3.55 us (2%)
    pallas_call x1, Pallas kernels, local(): pl.pallas_call(functools.partial(close_kernel, nx, ny, len(plan)), out_sh...  71.5 us
    pallas_call x1, Pallas kernels, local(): pl.pallas_call(functools.partial(open_kernel, nx, ny), out_shape=halo_sha...  43.6 us
    pallas_call x1, Pallas kernels, local(): pl.pallas_call(functools.partial(forward_kernel, width_x, width_y), out_s...  32.8 us
    pallas_call x1, Pallas kernels, local(): pl.pallas_call(functools.partial(backward_kernel, width_x, width_y, nx *...  17.7 us

profile of v1, /device:TPU:0, one launch (start us, length us, event | category | flops | bytes accessed | tf_op | source)
XLA Modules:
  0.0 171.0 jit_solution(15192256232956480355)
XLA Ops:
  0.6 0.8 reshape.100.occupancy
  1.4 0.8 reshape.101.offsets
  2.2 0.7 broadcast_multiply_fusion
  2.9 0.1 mul.35
  3.0 0.2 convert_reduce_fusion.rank
  3.2 0.1 add.51
  3.3 0.2 convert_reduce_fusion.1.rank
  3.4 0.1 select_reduce_fusion.order
  3.6 0.0 copy-start.1
  3.6 1.0 copy-done.1
  4.6 43.6 %open_exchange.1 = (bf16[2,4,512,128]{3,2,1,0:T(8,128)(2,1)}, bf16[2,4,512,128]{3,2,1,0:T(8,128)(2,1)}, bf16[4,512,128]{2,1,0:T(8,128)(2,1)S(1)}, bf16[8,2,64,256]{3,2,1,0:T(8,128)(2,1)S(1)}) custom-call(s32[16]{0:T(128)S(1)} %select_reduce_fusion.order, bf16[4,4,512,128]{3,2,1,0:T(8,128)(2,1)} %features.3, bf16[16,64,256]{2,1,0:T(8,128)(2,1)S(1)} %bitcast.7), custom_call_target="tpu_custom_call" | custom-call | tf_op jit(solution)/shard_map/open_exchange/pallas_call | solution.py:529
  48.2 0.0 copy-start
  48.3 0.8 copy-done
  49.0 32.8 %forward.1 = (bf16[16,512,128]{2,1,0:T(8,128)(2,1)}, bf16[16,64,256]{2,1,0:T(8,128)(2,1)S(1)}, f32[5632,128]{1,0:T(8,128)}, bf16[1024,256]{1,0:T(8,128)(2,1)S(1)}) custom-call(s32[16]{0:T(128)S(1)} %reshape.100.occupancy, s32[144]{0:T(256)S(1)} %reshape.101.offsets, s32[16]{0:T(128)S(1)} %convert_reduce_fusion.rank, bf16[4,4,512,128]{3,2,1,0:T(8,128)(2,1)} %features.3, ...), custom_call_target="tpu_custom_call" | custom-call | tf_op jit(solution)/shard_map/forward/pallas_call | solution.py:550
  81.8 71.5 %close_exchange.1 = (bf16[2,4,512,128]{3,2,1,0:T(8,128)(2,1)}, bf16[2,4,512,128]{3,2,1,0:T(8,128)(2,1)}, bf16[4,512,128]{2,1,0:T(8,128)(2,1)S(1)}, bf16[8,2,64,256]{3,2,1,0:T(8,128)(2,1)S(1)}, bf16[5632,128]{1,0:T(8,128)(2,1)}) custom-call(bf16[4,4,512,128]{3,2,1,0:T(8,128)(2,1)} %bitcast.9, bf16[8,2,64,256]{3,2,1,0:T(8,128)(2,1)S(1)} %bitcast.8, ...), custom_call_target="tpu_custom_call" | custom-call | tf_op jit(solution)/shard_map/close_exchange/pallas_call | solution.py:592
  153.4 17.7 %backward.1 = (bf16[4,4,64,256]{3,2,1,0:T(8,128)(2,1)}, bf16[4,4,512,128]{3,2,1,0:T(8,128)(2,1)}, f32[27,128,128]{2,1,0:T(8,128)}, f32[1024,256]{1,0:T(8,128)}) custom-call(s32[16]{0:T(128)S(1)} %reshape.100.occupancy, s32[144]{0:T(256)S(1)} %reshape.101.offsets, s32[16]{0:T(128)S(1)} %convert_reduce_fusion.1.rank, bf16[4,4,512,128]{3,2,1,0:T(8,128)(2,1)} %bitcast.10, ...), custom_call_target="tpu_custom_call" | custom-call | tf_op jit(solution)/shard_map/backward/pallas_call | solution.py:618
  (2 shorter events, 0.0 us)
Async XLA Ops:
  3.6 1.1 copy-start.1
  48.2 0.8 copy-start

commit v2 on v1

v2 whole, which is shorter than its diff:
```python
import functools

import jax
import jax.numpy as jnp
from jax import lax
from jax.experimental import pallas as pl
from jax.experimental.pallas import tpu as pltpu
from jax.sharding import PartitionSpec as P

MESH = pl.DeviceIdType.MESH
E = 8
NEIGHBOURS = [(-1, -1), (-1, 0), (-1, 1), (0, -1), (0, 0), (0, 1), (1, -1), (1, 0), (1, 1)]
HALO = [k for k in range(9) if k != 4]
SEND_ORDER = [1, 7, 3, 5, 0, 2, 6, 8]
ALONG_Y = [3, 5]
ALONG_X = [1, 7, 0, 2, 6, 8]
F32 = jnp.float32
BF16 = jnp.bfloat16
VMEM_LIMIT = 58 * 1024 * 1024


def position():
    return lax.axis_index("gx"), lax.axis_index("gy")


def exists(nx, ny, gx, gy, k):
    dx, dy = NEIGHBOURS[k]
    x, y = gx + dx, gy + dy
    return (x >= 0) & (x < nx) & (y >= 0) & (y < ny)


def edge(ref, width_x, width_y, k):
    dx, dy = NEIGHBOURS[k]
    sx = {-1: 0, 0: slice(None), 1: width_x - 1}[dx]
    sy = {-1: 0, 0: slice(None), 1: width_y - 1}[dy]
    return ref.at[sx, sy]


def slot(halo, k):
    hx, hy, hc = halo
    dx, dy = NEIGHBOURS[k]
    if dy == 0:
        return hx.at[(dx + 1) // 2]
    if dx == 0:
        return hy.at[(dy + 1) // 2]
    return hc.at[(dx + 1) // 2 * 2 + (dy + 1) // 2]


def halo_copy(nx, ny, gx, gy, source, halo, send, recv, k):
    dx, dy = NEIGHBOURS[k]
    return pltpu.make_async_remote_copy(
        src_ref=edge(source, source.shape[0], source.shape[1], k),
        dst_ref=slot(halo, 8 - k),
        send_sem=send.at[k],
        recv_sem=recv.at[8 - k],
        device_id=(gx + dx, gy + dy),
        device_id_type=MESH,
    )


def halo_arrival(nx, ny, gx, gy, source, halo, send, recv, k):
    dx, dy = NEIGHBOURS[k]
    return pltpu.make_async_remote_copy(
        src_ref=edge(source, source.shape[0], source.shape[1], 8 - k),
        dst_ref=slot(halo, k),
        send_sem=send.at[8 - k],
        recv_sem=recv.at[k],
        device_id=(gx + dx, gy + dy),
        device_id_type=MESH,
    )


def halo_fill(source, halo, recv, k):
    return pltpu.make_async_copy(
        edge(source, source.shape[0], source.shape[1], k), slot(halo, k), recv.at[k]
    )


def start_halo(nx, ny, gx, gy, source, halo, send, recv):
    for k in SEND_ORDER:
        there = exists(nx, ny, gx, gy, k)

        @pl.when(there)
        def _(k=k):
            halo_copy(nx, ny, gx, gy, source, halo, send, recv, k).start()

        @pl.when(jnp.logical_not(there))
        def _(k=k):
            halo_fill(source, halo, recv, k).start()


def finish_halo(nx, ny, gx, gy, source, halo, send, recv, chosen):
    for k in chosen:
        there = exists(nx, ny, gx, gy, k)

        @pl.when(there)
        def _(k=k):
            halo_copy(nx, ny, gx, gy, source, halo, send, recv, k).wait_send()
            halo_arrival(nx, ny, gx, gy, source, halo, send, recv, k).wait_recv()

        @pl.when(jnp.logical_not(there))
        def _(k=k):
            halo_fill(source, halo, recv, k).wait()


def exchange_copy(nx, gx, gy, outgoing, incoming, send, recv, shift):
    peer = lax.rem(gx + shift, nx)
    return pltpu.make_async_remote_copy(
        src_ref=outgoing.at[peer],
        dst_ref=incoming.at[gx],
        send_sem=send.at[shift],
        recv_sem=recv.at[shift],
        device_id=(peer, gy),
        device_id_type=MESH,
    )


def exchange_arrival(nx, gx, gy, outgoing, incoming, send, recv, shift):
    peer = lax.rem(gx + nx - shift, nx)
    return pltpu.make_async_remote_copy(
        src_ref=outgoing.at[peer],
        dst_ref=incoming.at[peer],
        send_sem=send.at[shift],
        recv_sem=recv.at[shift],
        device_id=(peer, gy),
        device_id_type=MESH,
    )


def start_exchange(nx, gx, gy, outgoing, incoming, send, recv):
    pltpu.make_async_copy(outgoing.at[gx], incoming.at[gx], recv.at[0]).start()
    for shift in range(1, nx):
        exchange_copy(nx, gx, gy, outgoing, incoming, send, recv, shift).start()


def finish_exchange(nx, gx, gy, outgoing, incoming, send, recv):
    pltpu.make_async_copy(outgoing.at[gx], incoming.at[gx], recv.at[0]).wait()
    for shift in range(1, nx):
        exchange_copy(nx, gx, gy, outgoing, incoming, send, recv, shift).wait_send()
        exchange_arrival(nx, gx, gy, outgoing, incoming, send, recv, shift).wait_recv()


def greet(nx, ny, gx, gy, partners):
    barrier = pltpu.get_barrier_semaphore()
    for k in HALO:
        dx, dy = NEIGHBOURS[k]

        @pl.when(exists(nx, ny, gx, gy, k))
        def _(dx=dx, dy=dy):
            pl.semaphore_signal(
                barrier, inc=1, device_id=(gx + dx, gy + dy), device_id_type=MESH
            )

    for shift in range(1, nx):
        pl.semaphore_signal(
            barrier, inc=1, device_id=(lax.rem(gx + shift, nx), gy), device_id_type=MESH
        )
    for partner in partners:
        pl.semaphore_signal(barrier, inc=1, device_id=partner, device_id_type=MESH)
    count = nx - 1 + len(partners)
    for k in HALO:
        count = count + jnp.where(exists(nx, ny, gx, gy, k), 1, 0)
    pl.semaphore_wait(barrier, count)


def groups(nx, ny):
    deep = 4 if nx % 4 == 0 else 1
    return [
        (axis, stride, size)
        for axis, stride, size in (
            (1, 1, 2),
            (1, 2, ny // 2),
            (0, 1, nx // deep),
            (0, nx // deep, deep),
        )
        if size > 1
    ]


def member(gx, gy, group, shift):
    axis, stride, size = group
    here = (gx, gy)[axis]
    own = lax.rem(lax.div(here, stride), size)
    other = lax.rem(own + shift, size)
    there = here + (other - own) * stride
    return own, other, ((there, gy) if axis == 0 else (gx, there))


def reduce_all(nx, ny, gx, gy, partial, total, sends, recvs, ss, rs, gs, gr, fill):
    rows = partial.shape[0]
    plan = groups(nx, ny)
    base, length = 0, rows
    bases = []
    sem = 0
    for stage, group in enumerate(plan):
        size = group[2]
        chunk = length // size
        copies = []
        own = None
        for shift in range(1, size):
            own, other, device = member(gx, gy, group, shift)
            start = pl.multiple_of(base + other * chunk, 16)
            sends[stage][shift - 1] = partial[pl.ds(start, chunk)].astype(BF16)
            copy = pltpu.make_async_remote_copy(
                src_ref=sends[stage].at[shift - 1],
                dst_ref=recvs[stage].at[shift - 1],
                send_sem=ss.at[sem],
                recv_sem=rs.at[sem],
                device_id=device,
                device_id_type=MESH,
            )
            copy.start()
            copies.append(copy)
            sem += 1
        bases.append(base)
        base = pl.multiple_of(base + own * chunk, 16)
        length = chunk
        fill("scatter", stage)
        for copy in copies:
            copy.wait()
        value = partial[pl.ds(base, chunk)]
        for shift in range(1, size):
            value = value + recvs[stage][shift - 1].astype(F32)
        partial[pl.ds(base, chunk)] = value
    total[pl.ds(base, length)] = (partial[pl.ds(base, length)]).astype(BF16)
    sem = 0
    for stage in reversed(range(len(plan))):
        group = plan[stage]
        size = group[2]
        copies = []
        for shift in range(1, size):
            own, other, device = member(gx, gy, group, shift)
            back = lax.rem(own + size - shift, size)
            copies.append(
                (
                    pltpu.make_async_remote_copy(
                        src_ref=total.at[pl.ds(base, length)],
                        dst_ref=total.at[pl.ds(base, length)],
                        send_sem=gs.at[sem],
                        recv_sem=gr.at[sem],
                        device_id=device,
                        device_id_type=MESH,
                    ),
                    pl.multiple_of(bases[stage] + back * length, 16),
                    sem,
                    device,
                )
            )
            copies[-1][0].start()
            sem += 1
        fill("gather", stage)
        for copy, start, index, device in copies:
            copy.wait_send()
            pltpu.make_async_remote_copy(
                src_ref=total.at[pl.ds(base, length)],
                dst_ref=total.at[pl.ds(start, length)],
                send_sem=gs.at[index],
                recv_sem=gr.at[index],
                device_id=device,
                device_id_type=MESH,
            ).wait_recv()
        base = bases[stage]
        length = length * size


def ext_source(width_x, width_y, refs, x, y):
    own, hx, hy, hc = refs
    sx = 0 if x < 0 else (2 if x >= width_x else 1)
    sy = 0 if y < 0 else (2 if y >= width_y else 1)
    if sx == 1 and sy == 1:
        return own, (x, y)
    if sy == 1:
        return hx, (sx // 2, y)
    if sx == 1:
        return hy, (sy // 2, x)
    return hc, (sx // 2 * 2 + sy // 2,)


def voxel_order(transposed):
    row = lax.broadcasted_iota(jnp.int32, (E**3, E**3), 1 if transposed else 0)
    column = lax.broadcasted_iota(jnp.int32, (E**3, E**3), 0 if transposed else 1)
    sub, cell = row // 64, row % 64
    a = (cell // 16) * 2 + sub // 4
    b = (cell // 4) % 4 * 2 + (sub // 2) % 2
    c = cell % 4 * 2 + sub % 2
    return jnp.where(column == (a * 8 + b) * 8 + c, 1.0, 0.0).astype(BF16)


def dot(a, b, dims):
    return lax.dot_general(a, b, (dims, ((), ())), preferred_element_type=F32)


def whole_kernel(
    nx,
    ny,
    stages,
    occupancy,
    offsets,
    send_rank,
    send_order,
    cell_rank,
    cell_order,
    features,
    cotangent,
    w_sub,
    w_down,
    coarse,
    feature_grad,
    sub_grad,
    down_grad,
    *scratch,
):
    sends, recvs = scratch[:stages], scratch[stages : 2 * stages]
    (
        hx, hy, hc, gx_halo, gy_halo, gc_halo,
        outgoing, incoming, leaving, arrived,
        pre_grad, ext, ext_t, weights, back_weights, preact, patches, hidden_grad,
        returned, shifted, partial, total,
        hs, hr, es, er, ps, pr, ms, mr, ss, rs, gs, gr,
    ) = scratch[2 * stages :]
    width_x, width_y = features.shape[:2]
    bricks = width_x * width_y
    wide = width_y + 2
    share = outgoing.shape[1]
    gx, gy = position()
    halo = (hx, hy, hc)
    grad_halo = (gx_halo, gy_halo, gc_halo)
    plan = groups(nx, ny)
    partners = [
        member(gx, gy, group, shift)[2] for group in plan for shift in range(1, group[2])
    ]
    greet(nx, ny, gx, gy, partners)
    start_halo(nx, ny, gx, gy, features, halo, hs, hr)
    for i in range(bricks):
        outgoing[i // share, i % share] = cotangent[cell_order[i]]
    start_exchange(nx, gx, gy, outgoing, incoming, es, er)

    order = voxel_order(False)
    cells = [(x, y) for x in range(-1, width_x + 1) for y in range(-1, width_y + 1)]
    own = [(x, y) for x, y in cells if 0 <= x < width_x and 0 <= y < width_y]
    beside = [(x, y) for x, y in cells if 0 <= x < width_x and not 0 <= y < width_y]
    outer_rows = [(x, y) for x, y in cells if not 0 <= x < width_x]

    def place(refs, chosen):
        for first in range(0, len(chosen), 2):
            pair = []
            for x, y in chosen[first : first + 2]:
                ref, at = ext_source(width_x, width_y, refs, x, y)
                pair.append(ref[at])
            both = dot(order, jnp.concatenate(pair, 1), ((1,), (0,))).astype(BF16)
            for j, (x, y) in enumerate(chosen[first : first + 2]):
                column = both[:, j * 128 : (j + 1) * 128]
                i = (x + 1) * wide + y + 1
                ext[i] = column
                ext_t[i] = column.T

    refs = (features, hx, hy, hc)
    place(refs, own)
    partial[...] = jnp.zeros_like(partial)
    finish_exchange(nx, gx, gy, outgoing, incoming, es, er)
    for p in range(bricks):
        rank = send_rank[p]
        returned[pl.ds(p * 64, 64)] = incoming[rank // share, rank % share]

    def spread(g, _):
        rows = pl.ds(pl.multiple_of(g * 256, 256), 256)
        hidden_grad[rows] = dot(returned[rows], w_down[...], ((1,), (1,)))
        return 0

    lax.fori_loop(0, bricks // 4, spread, 0)
    finish_halo(nx, ny, gx, gy, features, halo, hs, hr, ALONG_Y)
    place(refs, beside)

    def windows(p):
        x, y = p // width_y, p % width_y
        return x, y, [(x + 1 + dx) * wide + y + 1 + dy for dx, dy in NEIGHBOURS]

    def forward(p):
        x, y, at = windows(p)
        rows = pl.ds(pl.multiple_of(p * 64, 64), 64)
        present = occupancy[p].astype(F32)
        for k in range(9):
            code = offsets[p * 9 + k]
            chosen = w_sub[jnp.minimum(code, 26)]
            weights[pl.ds(k * 128, 128)] = jnp.where(code < 27, chosen, jnp.zeros_like(chosen))
        window = jnp.concatenate([ext[i] for i in at], 1)
        preact[...] = dot(window, weights[...], ((1,), (0,)))
        for s in range(8):
            part = pl.ds(s * 64, 64)
            lanes = pl.ds(s * 128, 128)
            pre = preact[part]
            sig = jax.nn.sigmoid(pre)
            centre = ext[at[4], part].astype(F32)
            patches[rows, lanes] = (present * (centre + pre * sig)).astype(BF16)
            slope = sig * (1.0 + pre * (1.0 - sig))
            pre_grad[x, y, part] = (present * hidden_grad[rows, lanes] * slope).astype(BF16)

    def kernel_grad(p):
        x, y, at = windows(p)
        window_t = jnp.concatenate([ext_t[i] for i in at], 0)
        outer = dot(window_t, pre_grad[x, y], ((1,), (0,)))
        for k in range(9):
            code = offsets[p * 9 + k]
            term = outer[k * 128 : (k + 1) * 128]
            for o in range(3 * k, 3 * k + 3):
                here = pl.ds(o * 128, 128)
                partial[here] = partial[here] + jnp.where(code == o, term, jnp.zeros_like(term))

    def inner_step(i, _):
        forward(i + width_y)
        kernel_grad(i + width_y)
        return 0

    middle = bricks - 2 * width_y
    lax.fori_loop(0, middle, inner_step, 0)
    finish_halo(nx, ny, gx, gy, features, halo, hs, hr, ALONG_X)
    place(refs, outer_rows)

    def rim(i):
        return i + (i // width_y) * middle

    def rim_forward(i, _):
        forward(rim(i))
        return 0

    lax.fori_loop(0, 2 * width_y, rim_forward, 0)
    start_halo(nx, ny, gx, gy, pre_grad, grad_halo, ps, pr)

    down = dot(patches[...], w_down[...], ((1,), (0,))).astype(BF16)
    for p in range(bricks):
        shifted[p] = down[p * 64 : (p + 1) * 64]
    for i in range(bricks):
        leaving[i // share, i % share] = shifted[send_order[i]]
    start_exchange(nx, gx, gy, leaving, arrived, ms, mr)

    def rim_grad(i, _):
        kernel_grad(rim(i))
        return 0

    lax.fori_loop(0, 2 * width_y, rim_grad, 0)
    top = 27 * 128
    for s in range(8):
        grad = dot(patches[:, s * 128 : (s + 1) * 128], returned[...], ((0,), (0,)))
        for half in range(2):
            partial[pl.ds(top + half * 1024 + s * 128, 128)] = grad[:, half * 128 : half * 128 + 128]

    back = voxel_order(True)
    grad_refs = (pre_grad, gx_halo, gy_halo, gc_halo)

    def lay(chosen):
        for x, y in chosen:
            ref, at = ext_source(width_x, width_y, grad_refs, x, y)
            ext[(x + 1) * wide + y + 1] = ref[at]

    def column(p):
        x, y, at = windows(p)
        for k in range(9):
            code = offsets[p * 9 + k]
            chosen = w_sub[jnp.maximum(26 - code, 0)]
            back_weights[:, k * 128 : (k + 1) * 128] = jnp.where(
                code < 27, chosen, jnp.zeros_like(chosen)
            )
        window = jnp.concatenate([ext[i] for i in at], 1)
        conv = dot(window, back_weights[...], ((1,), (1,)))
        rows = pl.ds(pl.multiple_of(p * 64, 64), 64)
        spread_rows = jnp.concatenate(
            [hidden_grad[rows, s * 128 : (s + 1) * 128] for s in range(8)], 0
        )
        return (occupancy[p].astype(F32) * (spread_rows + conv)).astype(BF16)

    def pair(i, _):
        p = i * 2
        both = jnp.concatenate([column(p), column(p + 1)], 1)
        out = dot(back, both, ((1,), (0,))).astype(BF16)
        feature_grad[p // width_y, p % width_y] = out[:, :128]
        feature_grad[(p + 1) // width_y, (p + 1) % width_y] = out[:, 128:]
        return 0

    per_row = width_y // 2
    last = bricks // 2
    half = last // 2

    def fill(phase, stage):
        if phase == "scatter" and stage == 0:
            lay(own)
            finish_halo(nx, ny, gx, gy, pre_grad, grad_halo, ps, pr, ALONG_Y)
            lay(beside)
        if phase == "scatter" and stage == 1:
            lax.fori_loop(per_row, last - per_row, pair, 0)
        if phase == "gather" and stage == 1:
            finish_halo(nx, ny, gx, gy, pre_grad, grad_halo, ps, pr, ALONG_X)
            lay(outer_rows)

            def rim_pair(i, _):
                return pair(i + (i // per_row) * (last - 2 * per_row), 0)

            lax.fori_loop(0, 2 * per_row, rim_pair, 0)
        if phase == "gather" and stage == 0:
            finish_exchange(nx, gx, gy, leaving, arrived, ms, mr)
            for p in range(bricks):
                rank = cell_rank[p]
                coarse[p // width_y, p % width_y] = arrived[rank // share, rank % share]

    reduce_all(nx, ny, gx, gy, partial, total, sends, recvs, ss, rs, gs, gr, fill)
    scale = 1.0 / (nx * ny)
    for o in range(27):
        sub_grad[o] = total[pl.ds(o * 128, 128)].astype(F32) * scale
    for side in range(2):
        down_grad[:, pl.ds(side * 128, 128)] = (
            total[pl.ds(top + side * 1024, 1024)].astype(F32) * scale
        )


def ranks(keys):
    rank = jnp.sum((keys[None, :] < keys[:, None]).astype(jnp.int32), 1)
    places = jnp.arange(keys.shape[0], dtype=jnp.int32)
    order = jnp.sum((rank[None, :] == places[:, None]).astype(jnp.int32) * places[None, :], 1)
    return rank, order


def local(nx, ny, features, occupancy, pair_offset, owner, w_sub, w_down, cotangent):
    width_x, width_y, voxels, channels = features.shape
    bricks = width_x * width_y
    cells, out_channels = cotangent.shape[2:]
    share = bricks // nx
    occupied = occupancy.reshape(bricks)
    offsets = pair_offset.reshape(bricks * 9)
    targets = owner.reshape(bricks)
    places = jnp.arange(bricks, dtype=jnp.int32)
    source = (2 * lax.axis_index("gx") - targets + nx) % nx
    send_rank, send_order = ranks(targets * bricks + places)
    cell_rank, cell_order = ranks(source * bricks + places)

    vmem = pl.BlockSpec(memory_space=pltpu.VMEM)
    smem = pl.BlockSpec(memory_space=pltpu.SMEM)
    shape = jax.ShapeDtypeStruct
    dma = pltpu.SemaphoreType.DMA
    halo_buffers = [
        pltpu.VMEM((2, width_y, voxels, channels), BF16),
        pltpu.VMEM((2, width_x, voxels, channels), BF16),
        pltpu.VMEM((4, voxels, channels), BF16),
    ]
    block = pltpu.VMEM((nx, share, cells, out_channels), BF16)
    unit = 16 * nx * ny
    rows = -(-(27 * channels + 2048) // unit) * unit
    plan = groups(nx, ny)
    buffers = []
    length = rows
    count = 0
    for _, _, size in plan:
        length //= size
        buffers.append(pltpu.VMEM((size - 1, length, 128), BF16))
        count += size - 1
    around = (width_x + 2) * (width_y + 2)
    return pl.pallas_call(
        functools.partial(whole_kernel, nx, ny, len(plan)),
        out_shape=[
            shape(cotangent.shape, BF16),
            shape(features.shape, BF16),
            shape(w_sub.shape, F32),
            shape(w_down.shape, F32),
        ],
        in_specs=[smem] * 6 + [vmem] * 4,
        out_specs=[vmem] * 4,
        scratch_shapes=buffers
        + buffers
        + halo_buffers
        + halo_buffers
        + [block] * 4
        + [
            pltpu.VMEM(features.shape, BF16),
            pltpu.VMEM((around, voxels, channels), BF16),
            pltpu.VMEM((around, channels, voxels), BF16),
            pltpu.VMEM((9 * channels, channels), BF16),
            pltpu.VMEM((channels, 9 * channels), BF16),
            pltpu.VMEM((voxels, channels), F32),
            pltpu.VMEM((bricks * cells, 8 * channels), BF16),
            pltpu.VMEM((bricks * cells, 8 * channels), F32),
            pltpu.VMEM((bricks * cells, out_channels), BF16),
            pltpu.VMEM((bricks, cells, out_channels), BF16),
            pltpu.VMEM((rows, 128), F32),
            pltpu.VMEM((rows, 128), BF16),
        ]
        + [dma((9,)), dma((9,)), dma((nx,)), dma((nx,))] * 2
        + [dma((count,))] * 4,
        compiler_params=pltpu.CompilerParams(
            collective_id=0, has_side_effects=True, vmem_limit_bytes=VMEM_LIMIT
        ),
        name="section",
    )(
        occupied,
        offsets,
        send_rank,
        send_order,
        cell_rank,
        cell_order,
        features,
        cotangent.reshape(bricks, cells, out_channels),
        w_sub,
        w_down,
    )


def solution(mesh):
    in_specs = (
        P("gx", "gy", None, None),
        P("gx", "gy"),
        P("gx", "gy", None),
        P("gx", "gy"),
        P(),
        P(),
        P("gx", "gy", None, None),
    )
    out_specs = (P("gx", "gy", None, None), P("gx", "gy", None, None), P(), P())
    return jax.shard_map(
        functools.partial(local, mesh.shape["gx"], mesh.shape["gy"]),
        mesh=mesh,
        in_specs=in_specs,
        out_specs=out_specs,
        check_vma=False,
    )
```

time: 171 us -> 147 us (0.86)
  Pallas kernels: 166 us -> 133 us
  local copies, waits for them, and re-layouts: 3.55 us -> 10.8 us
    pallas_call x4 -> x1, Pallas kernels: 166 us -> 133 us  [local(): pl.pallas_call(functools.partial(whole_kernel, nx, ny, len(plan)), out_sh...]
    unnamed x4 -> x12, local copies, waits for them, and re-layouts: 1.83 us -> 7.97 us
where the time goes in v2:
time: 147 us; the launch traced here: 146 us
  Pallas kernels  133 us (90%)
  local copies, waits for them, and re-layouts  10.8 us (7%)
  other arithmetic  1.77 us (1%)
    pallas_call x1, Pallas kernels, local(): pl.pallas_call(functools.partial(whole_kernel, nx, ny, len(plan)), out_sh...  133 us
    unnamed x12, local copies, waits for them, and re-layouts  7.97 us

profile of v2, /device:TPU:0, one launch (start us, length us, event | category | flops | bytes accessed | tf_op | source)
XLA Modules:
  0.0 146.2 jit_solution(4965972689276024593)
XLA Ops:
  0.6 1.3 reshape.88.occupancy
  1.9 1.4 reshape.89.offsets
  3.3 0.7 subtract_add_fusion
  3.9 0.1 add.52
  4.0 0.2 convert_reduce_fusion.cell_rank
  4.2 0.0 copy-start.2
  4.2 0.1 mul.42
  4.3 0.2 convert_reduce_fusion.1.send_rank
  4.5 0.0 copy-start.3
  4.5 0.7 select_reduce_fusion
  5.2 0.0 copy-done.2
  5.2 0.0 copy-done.3
  5.2 133.0 %section.1 = (bf16[4,4,64,256]{3,2,1,0:T(8,128)(2,1)}, bf16[4,4,512,128]{3,2,1,0:T(8,128)(2,1)}, f32[27,128,128]{2,1,0:T(8,128)}, f32[1024,256]{1,0:T(8,128)}) custom-call(s32[16]{0:T(128)} %reshape.88.occupancy, s32[144]{0:T(256)} %reshape.89.offsets, s32[16]{0:T(128)} %copy-done.3, s32[16]{0:T(128)} %get-tuple-element.7.send_order, s32[16]{0:T(128)} %copy-done.2, ...), custom_call_target="tpu_custom_call" | custom-call | tf_op jit(solution)/shard_map/section/pallas_call | solution.py:555
  138.2 1.9 %copy.15 = bf16[4,4,64,256]{3,2,1,0:T(8,128)(2,1)} copy(bf16[4,4,64,256]{3,2,1,0:T(8,128)(2,1)} %get-tuple-element.12) | data formatting | bytes 1048576
  140.1 0.0 copy-start
  140.1 3.2 %copy.16 = bf16[4,4,512,128]{3,2,1,0:T(8,128)(2,1)} copy(bf16[4,4,512,128]{3,2,1,0:T(8,128)(2,1)} %get-tuple-element.13) | data formatting | bytes 4194304
  143.4 0.0 copy-done
  143.4 0.0 copy-start.1
  143.4 1.2 copy.17
  144.6 0.7 copy-done.1
  145.2 1.0 copy.18
  (2 shorter events, 0.0 us)
Async XLA Ops:
  4.2 1.0 copy-start.2
  4.5 0.7 copy-start.3
  140.1 3.2 %copy-start = (f32[27,128,128]{2,1,0:T(8,128)S(1)}, f32[27,128,128]{2,1,0:T(8,128)}, u32[]{:S(2)}) copy-start(f32[27,128,128]{2,1,0:T(8,128)} %get-tuple-element.14) | copy-start | bytes 5308420
  143.4 1.9 %copy-start.1 = (f32[1024,256]{1,0:T(8,128)S(1)}, f32[1024,256]{1,0:T(8,128)}, u32[]{:S(2)}) copy-start(f32[1024,256]{1,0:T(8,128)} %get-tuple-element.15) | copy-start | bytes 3145732

commit v3 on v2

--- a/solution.py
+++ b/solution.py
@@ -10,10 +10,9 @@
 MESH = pl.DeviceIdType.MESH
 E = 8
 NEIGHBOURS = [(-1, -1), (-1, 0), (-1, 1), (0, -1), (0, 0), (0, 1), (1, -1), (1, 0), (1, 1)]
-HALO = [k for k in range(9) if k != 4]
-SEND_ORDER = [1, 7, 3, 5, 0, 2, 6, 8]
+ALONG_X = [1, 7]
 ALONG_Y = [3, 5]
-ALONG_X = [1, 7, 0, 2, 6, 8]
+HALO = ALONG_X + ALONG_Y
 F32 = jnp.float32
 BF16 = jnp.bfloat16
 VMEM_LIMIT = 58 * 1024 * 1024
@@ -76,8 +75,8 @@
     )
 
 
-def start_halo(nx, ny, gx, gy, source, halo, send, recv):
-    for k in SEND_ORDER:
+def start_halo(nx, ny, gx, gy, source, halo, send, recv, chosen):
+    for k in chosen:
         there = exists(nx, ny, gx, gy, k)
 
         @pl.when(there)
@@ -101,6 +100,70 @@
         @pl.when(jnp.logical_not(there))
         def _(k=k):
             halo_fill(source, halo, recv, k).wait()
+
+
+def corner_copy(gx, gy, halo, send, recv, side, dy):
+    hx, _, hc = halo
+    dx = 2 * side - 1
+    column = 0 if dy < 0 else hx.shape[1] - 1
+    here, there = 3 * (dx + 1) + dy + 1, 3 * (dx + 1) - dy + 1
+    return pltpu.make_async_remote_copy(
+        src_ref=hx.at[side, column],
+        dst_ref=hc.at[2 * side + (1 - dy) // 2],
+        send_sem=send.at[here],
+        recv_sem=recv.at[there],
+        device_id=(gx, gy + dy),
+        device_id_type=MESH,
+    )
+
+
+def corner_arrival(gx, gy, halo, send, recv, side, dy):
+    hx, _, hc = halo
+    k = 3 * 2 * side + dy + 1
+    return pltpu.make_async_remote_copy(
+        src_ref=hx.at[side, 0],
+        dst_ref=hc.at[2 * side + (1 + dy) // 2],
+        send_sem=send.at[k],
+        recv_sem=recv.at[k],
+        device_id=(gx, gy + dy),
+        device_id_type=MESH,
+    )
+
+
+def corner_fill(halo, recv, side, dy):
+    hx, _, hc = halo
+    return pltpu.make_async_copy(
+        hx.at[side, 0], hc.at[2 * side + (1 + dy) // 2], recv.at[3 * 2 * side + dy + 1]
+    )
+
+
+def start_corners(ny, gx, gy, halo, send, recv):
+    for side in range(2):
+        for dy in (-1, 1):
+            there = (gy + dy >= 0) & (gy + dy < ny)
+
+            @pl.when(there)
+            def _(side=side, dy=dy):
+                corner_copy(gx, gy, halo, send, recv, side, dy).start()
+
+            @pl.when(jnp.logical_not(there))
+            def _(side=side, dy=dy):
+                corner_fill(halo, recv, side, dy).start()
+
+
+def finish_corners(ny, gx, gy, halo, send, recv):
+    for side in range(2):
+        for dy in (-1, 1):
+            there = (gy + dy >= 0) & (gy + dy < ny)
+
+            @pl.when(there)
+            def _(side=side, dy=dy):
+                corner_copy(gx, gy, halo, send, recv, side, dy).wait_send()
+                corner_arrival(gx, gy, halo, send, recv, side, dy).wait_recv()
+
+            @pl.when(jnp.logical_not(there))
+            def _(side=side, dy=dy):
+                corner_fill(halo, recv, side, dy).wait()
 
 
 def exchange_copy(nx, gx, gy, outgoing, incoming, send, recv, shift):
@@ -186,81 +249,96 @@
     return own, other, ((there, gy) if axis == 0 else (gx, there))
 
 
+def pieces(nx, ny, rows):
+    plan = groups(nx, ny)
+    unit = 16 * nx * ny
+    first = rows // unit // 2 * unit
+    turned = plan[:1] + plan[1:-1][::-1] + plan[-1:]
+    return [(0, first, plan), (first, rows - first, turned)]
+
+
 def reduce_all(nx, ny, gx, gy, partial, total, sends, recvs, ss, rs, gs, gr, fill):
-    rows = partial.shape[0]
-    plan = groups(nx, ny)
-    base, length = 0, rows
-    bases = []
+    work = pieces(nx, ny, partial.shape[0])
+    stages = len(work[0][2])
+    base = [start for start, _, _ in work]
+    length = [count for _, count, _ in work]
+    bases = [[] for _ in work]
     sem = 0
-    for stage, group in enumerate(plan):
-        size = group[2]
-        chunk = length // size
+    for stage in range(stages):
         copies = []
-        own = None
-        for shift in range(1, size):
-            own, other, device = member(gx, gy, group, shift)
-            start = pl.multiple_of(base + other * chunk, 16)
-            sends[stage][shift - 1] = partial[pl.ds(start, chunk)].astype(BF16)
-            copy = pltpu.make_async_remote_copy(
-                src_ref=sends[stage].at[shift - 1],
-                dst_ref=recvs[stage].at[shift - 1],
-                send_sem=ss.at[sem],
-                recv_sem=rs.at[sem],
-                device_id=device,
-                device_id_type=MESH,
-            )
-            copy.start()
-            copies.append(copy)
-            sem += 1
-        bases.append(base)
-        base = pl.multiple_of(base + own * chunk, 16)
-        length = chunk
+        for w, (_, _, plan) in enumerate(work):
+            group = plan[stage]
+            size = group[2]
+            chunk = length[w] // size
+            buffer = w * stages + stage
+            for shift in range(1, size):
+                own, other, device = member(gx, gy, group, shift)
+                start = pl.multiple_of(base[w] + other * chunk, 16)
+                sends[buffer][shift - 1] = partial[pl.ds(start, chunk)].astype(BF16)
+                copy = pltpu.make_async_remote_copy(
+                    src_ref=sends[buffer].at[shift - 1],
+                    dst_ref=recvs[buffer].at[shift - 1],
+                    send_sem=ss.at[sem],
+                    recv_sem=rs.at[sem],
+                    device_id=device,
+                    device_id_type=MESH,
+                )
+                copy.start()
+                copies.append(copy)
+                sem += 1
+            bases[w].append(base[w])
+            base[w] = pl.multiple_of(base[w] + own * chunk, 16)
+            length[w] = chunk
         fill("scatter", stage)
         for copy in copies:
             copy.wait()
-        value = partial[pl.ds(base, chunk)]
-        for shift in range(1, size):
-            value = value + recvs[stage][shift - 1].astype(F32)
-        partial[pl.ds(base, chunk)] = value
-    total[pl.ds(base, length)] = (partial[pl.ds(base, length)]).astype(BF16)
+        for w, (_, _, plan) in enumerate(work):
+            buffer = w * stages + stage
+            here = pl.ds(base[w], length[w])
+            value = partial[here]
+            for shift in range(1, plan[stage][2]):
+                value = value + recvs[buffer][shift - 1].astype(F32)
+            partial[here] = value
+    for w in range(len(work)):
+        here = pl.ds(base[w], length[w])
+        total[here] = partial[here].astype(BF16)
     sem = 0
-    for stage in reversed(range(len(plan))):
-        group = plan[stage]
-        size = group[2]
+    for stage in reversed(range(stages)):
         copies = []
-        for shift in range(1, size):
-            own, other, device = member(gx, gy, group, shift)
-            back = lax.rem(own + size - shift, size)
-            copies.append(
-                (
-                    pltpu.make_async_remote_copy(
-                        src_ref=total.at[pl.ds(base, length)],
-                        dst_ref=total.at[pl.ds(base, length)],
-                        send_sem=gs.at[sem],
-                        recv_sem=gr.at[sem],
-                        device_id=device,
-                        device_id_type=MESH,
-                    ),
-                    pl.multiple_of(bases[stage] + back * length, 16),
-                    sem,
-                    device,
+        for w, (_, _, plan) in enumerate(work):
+            group = plan[stage]
+            size = group[2]
+            here = pl.ds(base[w], length[w])
+            for shift in range(1, size):
+                own, other, device = member(gx, gy, group, shift)
+                back = lax.rem(own + size - shift, size)
+                landing = pl.multiple_of(bases[w][stage] + back * length[w], 16)
+                copy = pltpu.make_async_remote_copy(
+                    src_ref=total.at[here],
+                    dst_ref=total.at[here],
+                    send_sem=gs.at[sem],
+                    recv_sem=gr.at[sem],
+                    device_id=device,
+                    device_id_type=MESH,
                 )
-            )
-            copies[-1][0].start()
-            sem += 1
+                copy.start()
+                arrival = pltpu.make_async_remote_copy(
+                    src_ref=total.at[here],
+                    dst_ref=total.at[pl.ds(landing, length[w])],
+                    send_sem=gs.at[sem],
+                    recv_sem=gr.at[sem],
+                    device_id=device,
+                    device_id_type=MESH,
+                )
+                copies.append((copy, arrival))
+                sem += 1
         fill("gather", stage)
-        for copy, start, index, device in copies:
+        for copy, arrival in copies:
             copy.wait_send()
-            pltpu.make_async_remote_copy(
-                src_ref=total.at[pl.ds(base, length)],
-                dst_ref=total.at[pl.ds(start, length)],
-                send_sem=gs.at[index],
-                recv_sem=gr.at[index],
-                device_id=device,
-                device_id_type=MESH,
-            ).wait_recv()
-        base = bases[stage]
-        length = length * size
+            arrival.wait_recv()
+        for w, (_, _, plan) in enumerate(work):
+            base[w] = bases[w][stage]
+            length[w] = length[w] * plan[stage][2]
 
 
 def ext_source(width_x, width_y, refs, x, y):
@@ -306,18 +384,18 @@
     w_down,
     coarse,
     feature_grad,
-    sub_grad,
-    down_grad,
+    total,
     *scratch,
 ):
-    sends, recvs = scratch[:stages], scratch[stages : 2 * stages]
+    buffers = 2 * stages
+    sends, recvs = scratch[:buffers], scratch[buffers : 2 * buffers]
     (
         hx, hy, hc, gx_halo, gy_halo, gc_halo,
         outgoing, incoming, leaving, arrived,
         pre_grad, ext, ext_t, weights, back_weights, preact, patches, hidden_grad,
-        returned, shifted, partial, total,
+        returned, shifted, partial,
         hs, hr, es, er, ps, pr, ms, mr, ss, rs, gs, gr,
-    ) = scratch[2 * stages :]
+    ) = scratch[2 * buffers :]
     width_x, width_y = features.shape[:2]
     bricks = width_x * width_y
     wide = width_y + 2
@@ -330,7 +408,7 @@
         member(gx, gy, group, shift)[2] for group in plan for shift in range(1, group[2])
     ]
     greet(nx, ny, gx, gy, partners)
-    start_halo(nx, ny, gx, gy, features, halo, hs, hr)
+    start_halo(nx, ny, gx, gy, features, halo, hs, hr, HALO)
     for i in range(bricks):
         outgoing[i // share, i % share] = cotangent[cell_order[i]]
     start_exchange(nx, gx, gy, outgoing, incoming, es, er)
@@ -414,17 +492,32 @@
     middle = bricks - 2 * width_y
     lax.fori_loop(0, middle, inner_step, 0)
     finish_halo(nx, ny, gx, gy, features, halo, hs, hr, ALONG_X)
-    place(refs, outer_rows)
+    start_corners(ny, gx, gy, halo, hs, hr)
+    ahead = [(x, y) for x, y in outer_rows if 0 <= y < width_y]
+    corners = [(x, y) for x, y in outer_rows if not 0 <= y < width_y]
+    place(refs, ahead)
+    inside = width_y - 2
+    jump = (width_x - 1) * width_y
+
+    def rim_inside(i, _):
+        forward(i // inside * jump + 1 + i % inside)
+        return 0
+
+    lax.fori_loop(0, 2 * inside, rim_inside, 0)
+    finish_corners(ny, gx, gy, halo, hs, hr)
+    place(refs, corners)
+    for side in range(2):
+
+        def rim_ends(i, _, side=side):
+            forward(side * jump + i * (width_y - 1))
+            return 0
+
+        lax.fori_loop(0, 2, rim_ends, 0)
+        start_halo(nx, ny, gx, gy, pre_grad, grad_halo, ps, pr, ALONG_X[side : side + 1])
+    start_halo(nx, ny, gx, gy, pre_grad, grad_halo, ps, pr, ALONG_Y)
 
     def rim(i):
         return i + (i // width_y) * middle
-
-    def rim_forward(i, _):
-        forward(rim(i))
-        return 0
-
-    lax.fori_loop(0, 2 * width_y, rim_forward, 0)
-    start_halo(nx, ny, gx, gy, pre_grad, grad_halo, ps, pr)
 
     down = dot(patches[...], w_down[...], ((1,), (0,))).astype(BF16)
     for p in range(bricks):
@@ -487,9 +580,13 @@
             lay(beside)
         if phase == "scatter" and stage == 1:
             lax.fori_loop(per_row, last - per_row, pair, 0)
-        if phase == "gather" and stage == 1:
+        if phase == "gather" and stage == stages - 1:
             finish_halo(nx, ny, gx, gy, pre_grad, grad_halo, ps, pr, ALONG_X)
-            lay(outer_rows)
+            start_corners(ny, gx, gy, grad_halo, ps, pr)
+            lay(ahead)
+        if phase == "gather" and stage == stages - 2:
+            finish_corners(ny, gx, gy, grad_halo, ps, pr)
+            lay(corners)
 
             def rim_pair(i, _):
                 return pair(i + (i // per_row) * (last - 2 * per_row), 0)
@@ -502,13 +599,6 @@
                 coarse[p // width_y, p % width_y] = arrived[rank // share, rank % share]
 
     reduce_all(nx, ny, gx, gy, partial, total, sends, recvs, ss, rs, gs, gr, fill)
-    scale = 1.0 / (nx * ny)
-    for o in range(27):
-        sub_grad[o] = total[pl.ds(o * 128, 128)].astype(F32) * scale
-    for side in range(2):
-        down_grad[:, pl.ds(side * 128, 128)] = (
-            total[pl.ds(top + side * 1024, 1024)].astype(F32) * scale
-        )
 
 
 def ranks(keys):
@@ -543,25 +633,24 @@
     block = pltpu.VMEM((nx, share, cells, out_channels), BF16)
     unit = 16 * nx * ny
     rows = -(-(27 * channels + 2048) // unit) * unit
-    plan = groups(nx, ny)
+    stages = len(groups(nx, ny))
     buffers = []
-    length = rows
     count = 0
-    for _, _, size in plan:
-        length //= size
-        buffers.append(pltpu.VMEM((size - 1, length, 128), BF16))
-        count += size - 1
+    for _, length, plan in pieces(nx, ny, rows):
+        for _, _, size in plan:
+            length //= size
+            buffers.append(pltpu.VMEM((size - 1, length, 128), BF16))
+            count += size - 1
     around = (width_x + 2) * (width_y + 2)
-    return pl.pallas_call(
-        functools.partial(whole_kernel, nx, ny, len(plan)),
+    coarse, feature_grad, total = pl.pallas_call(
+        functools.partial(whole_kernel, nx, ny, stages),
         out_shape=[
             shape(cotangent.shape, BF16),
             shape(features.shape, BF16),
-            shape(w_sub.shape, F32),
-            shape(w_down.shape, F32),
+            shape((rows, 128), BF16),
         ],
         in_specs=[smem] * 6 + [vmem] * 4,
-        out_specs=[vmem] * 4,
+        out_specs=[vmem] * 3,
         scratch_shapes=buffers
         + buffers
         + halo_buffers
@@ -579,7 +668,6 @@
             pltpu.VMEM((bricks * cells, out_channels), BF16),
             pltpu.VMEM((bricks, cells, out_channels), BF16),
             pltpu.VMEM((rows, 128), F32),
-            pltpu.VMEM((rows, 128), BF16),
         ]
         + [dma((9,)), dma((9,)), dma((nx,)), dma((nx,))] * 2
         + [dma((count,))] * 4,
@@ -599,6 +687,12 @@
         w_sub,
         w_down,
     )
+    scale = 1.0 / (nx * ny)
+    top = 27 * channels
+    sides = total[top : top + 2048].reshape(2, 1024, 128)
+    sub_grad = total[:top].astype(F32).reshape(w_sub.shape) * scale
+    down_grad = jnp.concatenate([sides[0], sides[1]], 1).astype(F32) * scale
+    return coarse, feature_grad, sub_grad, down_grad
 
 
 def solution(mesh):

time: 147 us -> 133 us (0.905)
  Pallas kernels: 133 us -> 121 us
  local copies, waits for them, and re-layouts: 10.8 us -> 6.13 us
  other arithmetic: 1.77 us -> 5.31 us
    pallas_call x1, Pallas kernels: 133 us -> 121 us  [local(): pl.pallas_call(functools.partial(whole_kernel, nx, ny, stages), out_shape...]
    unnamed x12 -> x10, local copies, waits for them, and re-layouts: 7.97 us -> 2.13 us
    mul x0 -> x2, other arithmetic: none -> 3.55 us  [the longest x1 2.49 us: local(): sub_grad = total[:top].astype(F32).reshape(w_sub.shape) * scale]
where the time goes in v3:
time: 133 us
  Pallas kernels  121 us (91%)
  local copies, waits for them, and re-layouts  6.13 us (5%)
  other arithmetic  5.31 us (4%)
    pallas_call x1, Pallas kernels, local(): pl.pallas_call(functools.partial(whole_kernel, nx, ny, stages), out_shape...  121 us

profile of v3, /device:TPU:0, one launch (start us, length us, event | category | flops | bytes accessed | tf_op | source)
XLA Modules:
  0.0 132.9 jit_solution(3062128847725276608)
XLA Ops:
  0.6 1.3 reshape.96.occupancy
  1.9 1.4 %reshape.97.offsets = s32[144]{0:T(256)} reshape(s32[4,4,9]{2,1,0:T(4,128)} %param.9) | data formatting | bytes 1152 | tf_op jit(solution)/shard_map/reshape | solution.py:617
  3.3 0.7 subtract_add_fusion
  3.9 0.1 mul.57
  4.0 0.2 convert_reduce_fusion.1.send_rank
  4.2 0.0 copy-start.2
  4.2 0.1 add.52
  4.3 0.2 convert_reduce_fusion.cell_rank
  4.5 0.0 copy-start.3
  4.5 0.7 select_reduce_fusion
  5.2 0.0 copy-done.2
  5.2 0.0 copy-done.3
  5.2 120.8 %section.1 = (bf16[4,4,64,256]{3,2,1,0:T(8,128)(2,1)}, bf16[4,4,512,128]{3,2,1,0:T(8,128)(2,1)}, bf16[5632,128]{1,0:T(8,128)(2,1)}) custom-call(s32[16]{0:T(128)} %reshape.96.occupancy, s32[144]{0:T(256)} %reshape.97.offsets, s32[16]{0:T(128)} %copy-done.2, s32[16]{0:T(128)} %get-tuple-element.15.send_order, s32[16]{0:T(128)} %copy-done.3, ...), custom_call_target="tpu_custom_call" | custom-call | tf_op jit(solution)/shard_map/section/pallas_call | solution.py:645
  126.0 2.5 %convert_multiply_fusion = f32[3456,128]{1,0:T(8,128)} fusion(bf16[5632,128]{1,0:T(8,128)(2,1)} %get-tuple-element.9), kind=kLoop, calls=%fused_computation | loop fusion | flops 884736 | bytes 2654208 | tf_op jit(solution)/shard_map/mul | solution.py:693
  128.5 0.0 copy-start.1
  128.5 0.0 copy-start
  128.5 1.2 fusion.3
  129.7 1.1 convert_multiply_fusion.1
  130.8 0.0 copy-done.1
  130.8 0.8 copy.13
  131.6 0.0 copy-done
  131.6 1.3 copy.14
  (2 shorter events, 0.0 us)
Async XLA Ops:
  4.2 1.0 copy-start.2
  4.5 0.7 copy-start.3
  128.5 2.3 %copy-start.1 = (bf16[4,4,64,256]{3,2,1,0:T(8,128)(2,1)S(1)}, bf16[4,4,64,256]{3,2,1,0:T(8,128)(2,1)}, u32[]{:S(2)}) copy-start(bf16[4,4,64,256]{3,2,1,0:T(8,128)(2,1)} %get-tuple-element.20) | copy-start | bytes 1572868
  128.5 3.1 %copy-start = (bf16[4,4,512,128]{3,2,1,0:T(8,128)(2,1)S(1)}, bf16[4,4,512,128]{3,2,1,0:T(8,128)(2,1)}, u32[]{:S(2)}) copy-start(bf16[4,4,512,128]{3,2,1,0:T(8,128)(2,1)} %get-tuple-element.21) | copy-start | bytes 6291460

commit v4 on v3

--- a/solution.py
+++ b/solution.py
@@ -392,7 +392,7 @@
     (
         hx, hy, hc, gx_halo, gy_halo, gc_halo,
         outgoing, incoming, leaving, arrived,
-        pre_grad, ext, ext_t, weights, back_weights, preact, patches, hidden_grad,
+        pre_grad, ext, ext_t, weights, back_weights, preact, patches, hidden_grad, slopes,
         returned, shifted, partial,
         hs, hr, es, er, ps, pr, ms, mr, ss, rs, gs, gr,
     ) = scratch[2 * buffers :]
@@ -411,7 +411,6 @@
     start_halo(nx, ny, gx, gy, features, halo, hs, hr, HALO)
     for i in range(bricks):
         outgoing[i // share, i % share] = cotangent[cell_order[i]]
-    start_exchange(nx, gx, gy, outgoing, incoming, es, er)
 
     order = voxel_order(False)
     cells = [(x, y) for x in range(-1, width_x + 1) for y in range(-1, width_y + 1)]
@@ -435,17 +434,6 @@
     refs = (features, hx, hy, hc)
     place(refs, own)
     partial[...] = jnp.zeros_like(partial)
-    finish_exchange(nx, gx, gy, outgoing, incoming, es, er)
-    for p in range(bricks):
-        rank = send_rank[p]
-        returned[pl.ds(p * 64, 64)] = incoming[rank // share, rank % share]
-
-    def spread(g, _):
-        rows = pl.ds(pl.multiple_of(g * 256, 256), 256)
-        hidden_grad[rows] = dot(returned[rows], w_down[...], ((1,), (1,)))
-        return 0
-
-    lax.fori_loop(0, bricks // 4, spread, 0)
     finish_halo(nx, ny, gx, gy, features, halo, hs, hr, ALONG_Y)
     place(refs, beside)
 
@@ -471,7 +459,17 @@
             centre = ext[at[4], part].astype(F32)
             patches[rows, lanes] = (present * (centre + pre * sig)).astype(BF16)
             slope = sig * (1.0 + pre * (1.0 - sig))
-            pre_grad[x, y, part] = (present * hidden_grad[rows, lanes] * slope).astype(BF16)
+            slopes[p, part] = slope
+
+    def gradient(p, _):
+        x, y = p // width_y, p % width_y
+        rows = pl.ds(pl.multiple_of(p * 64, 64), 64)
+        present = occupancy[p].astype(F32)
+        for s in range(8):
+            part = pl.ds(s * 64, 64)
+            grad = present * hidden_grad[rows, s * 128 : (s + 1) * 128] * slopes[p, part]
+            pre_grad[x, y, part] = grad.astype(BF16)
+        return 0
 
     def kernel_grad(p):
         x, y, at = windows(p)
@@ -486,13 +484,13 @@
 
     def inner_step(i, _):
         forward(i + width_y)
-        kernel_grad(i + width_y)
         return 0
 
     middle = bricks - 2 * width_y
     lax.fori_loop(0, middle, inner_step, 0)
     finish_halo(nx, ny, gx, gy, features, halo, hs, hr, ALONG_X)
     start_corners(ny, gx, gy, halo, hs, hr)
+    start_exchange(nx, gx, gy, outgoing, incoming, es, er)
     ahead = [(x, y) for x, y in outer_rows if 0 <= y < width_y]
     corners = [(x, y) for x, y in outer_rows if not 0 <= y < width_y]
     place(refs, ahead)
@@ -513,24 +511,34 @@
             return 0
 
         lax.fori_loop(0, 2, rim_ends, 0)
-        start_halo(nx, ny, gx, gy, pre_grad, grad_halo, ps, pr, ALONG_X[side : side + 1])
-    start_halo(nx, ny, gx, gy, pre_grad, grad_halo, ps, pr, ALONG_Y)
-
-    def rim(i):
-        return i + (i // width_y) * middle
 
     down = dot(patches[...], w_down[...], ((1,), (0,))).astype(BF16)
     for p in range(bricks):
         shifted[p] = down[p * 64 : (p + 1) * 64]
     for i in range(bricks):
         leaving[i // share, i % share] = shifted[send_order[i]]
-    start_exchange(nx, gx, gy, leaving, arrived, ms, mr)
-
-    def rim_grad(i, _):
-        kernel_grad(rim(i))
+    finish_exchange(nx, gx, gy, outgoing, incoming, es, er)
+    for p in range(bricks):
+        rank = send_rank[p]
+        returned[pl.ds(p * 64, 64)] = incoming[rank // share, rank % share]
+
+    def spread(g, _):
+        rows = pl.ds(pl.multiple_of(g * 256, 256), 256)
+        hidden_grad[rows] = dot(returned[rows], w_down[...], ((1,), (1,)))
         return 0
 
-    lax.fori_loop(0, 2 * width_y, rim_grad, 0)
+    lax.fori_loop(0, bricks // 4, spread, 0)
+    for side in range(2):
+        lax.fori_loop(side * jump, side * jump + width_y, gradient, 0)
+        start_halo(nx, ny, gx, gy, pre_grad, grad_halo, ps, pr, ALONG_X[side : side + 1])
+    lax.fori_loop(width_y, bricks - width_y, gradient, 0)
+    start_halo(nx, ny, gx, gy, pre_grad, grad_halo, ps, pr, ALONG_Y)
+
+    def every_grad(p, _):
+        kernel_grad(p)
+        return 0
+
+    lax.fori_loop(0, bricks, every_grad, 0)
     top = 27 * 128
     for s in range(8):
         grad = dot(patches[:, s * 128 : (s + 1) * 128], returned[...], ((0,), (0,)))
@@ -583,6 +591,7 @@
         if phase == "gather" and stage == stages - 1:
             finish_halo(nx, ny, gx, gy, pre_grad, grad_halo, ps, pr, ALONG_X)
             start_corners(ny, gx, gy, grad_halo, ps, pr)
+            start_exchange(nx, gx, gy, leaving, arrived, ms, mr)
             lay(ahead)
         if phase == "gather" and stage == stages - 2:
             finish_corners(ny, gx, gy, grad_halo, ps, pr)
@@ -665,6 +674,7 @@
             pltpu.VMEM((voxels, channels), F32),
             pltpu.VMEM((bricks * cells, 8 * channels), BF16),
             pltpu.VMEM((bricks * cells, 8 * channels), F32),
+            pltpu.VMEM((bricks, voxels, channels), F32),
             pltpu.VMEM((bricks * cells, out_channels), BF16),
             pltpu.VMEM((bricks, cells, out_channels), BF16),
             pltpu.VMEM((rows, 128), F32),

time: 133 us -> 119 us (0.89)
  Pallas kernels: 121 us -> 107 us
    pallas_call x1, Pallas kernels: 121 us -> 107 us  [local(): pl.pallas_call(functools.partial(whole_kernel, nx, ny, stages), out_shape...]
where the time goes in v4:
time: 119 us
  Pallas kernels  107 us (90%)
  local copies, waits for them, and re-layouts  6.13 us (5%)
  other arithmetic  5.31 us (4%)
    pallas_call x1, Pallas kernels, local(): pl.pallas_call(functools.partial(whole_kernel, nx, ny, stages), out_shape...  107 us
    mul x1, other arithmetic, local(): sub_grad = total[:top].astype(F32).reshape(w_sub.shape) * scale  2.49 us

profile of v4, /device:TPU:0, one launch (start us, length us, event | category | flops | bytes accessed | tf_op | source)
XLA Modules:
  0.0 118.8 jit_solution(15269979268137797139)
XLA Ops:
  0.6 1.3 %reshape.96.occupancy = s32[16]{0:T(128)} reshape(s32[4,4]{1,0:T(4,128)} %param.8) | data formatting | bytes 128 | tf_op jit(solution)/shard_map/reshape | solution.py:625
  1.9 1.4 %reshape.97.offsets = s32[144]{0:T(256)} reshape(s32[4,4,9]{2,1,0:T(4,128)} %param.9) | data formatting | bytes 1152 | tf_op jit(solution)/shard_map/reshape | solution.py:626
  3.3 0.7 subtract_add_fusion
  3.9 0.1 mul.57
  4.0 0.2 convert_reduce_fusion.1.send_rank
  4.2 0.0 copy-start.2
  4.2 0.1 add.52
  4.3 0.2 convert_reduce_fusion.cell_rank
  4.5 0.0 copy-start.3
  4.5 0.7 select_reduce_fusion
  5.2 0.0 copy-done.2
  5.2 0.0 copy-done.3
  5.2 106.6 %section.1 = (bf16[4,4,64,256]{3,2,1,0:T(8,128)(2,1)}, bf16[4,4,512,128]{3,2,1,0:T(8,128)(2,1)}, bf16[5632,128]{1,0:T(8,128)(2,1)}) custom-call(s32[16]{0:T(128)} %reshape.96.occupancy, s32[144]{0:T(256)} %reshape.97.offsets, s32[16]{0:T(128)} %copy-done.2, s32[16]{0:T(128)} %get-tuple-element.15.send_order, s32[16]{0:T(128)} %copy-done.3, ...), custom_call_target="tpu_custom_call" | custom-call | tf_op jit(solution)/shard_map/section/pallas_call | solution.py:654
  111.9 2.5 %convert_multiply_fusion = f32[3456,128]{1,0:T(8,128)} fusion(bf16[5632,128]{1,0:T(8,128)(2,1)} %get-tuple-element.9), kind=kLoop, calls=%fused_computation | loop fusion | flops 884736 | bytes 2654208 | tf_op jit(solution)/shard_map/mul | solution.py:703
  114.4 0.0 copy-start.1
  114.4 0.0 copy-start
  114.4 1.2 %fusion.3 = (bf16[1024,128]{1,0:T(8,128)(2,1)S(1)}, bf16[1024,128]{1,0:T(8,128)(2,1)S(1)}) fusion(bf16[5632,128]{1,0:T(8,128)(2,1)} %get-tuple-element.9), kind=kLoop, calls=%fused_computation.17 | loop fusion | bytes 1048576 | tf_op jit(solution)/shard_map/slice | solution.py:704
  115.6 1.1 convert_multiply_fusion.1
  116.6 0.0 copy-done.1
  116.6 0.8 copy.13
  117.4 0.0 copy-done
  117.4 1.3 %copy.14 = bf16[4,4,512,128]{3,2,1,0:T(8,128)(2,1)} copy(bf16[4,4,512,128]{3,2,1,0:T(8,128)(2,1)S(1)} %copy-done) | data formatting | bytes 4194304
  (2 shorter events, 0.0 us)
Async XLA Ops:
  4.2 1.0 copy-start.2
  4.5 0.7 copy-start.3
  114.4 2.3 %copy-start.1 = (bf16[4,4,64,256]{3,2,1,0:T(8,128)(2,1)S(1)}, bf16[4,4,64,256]{3,2,1,0:T(8,128)(2,1)}, u32[]{:S(2)}) copy-start(bf16[4,4,64,256]{3,2,1,0:T(8,128)(2,1)} %get-tuple-element.20) | copy-start | bytes 1572868
  114.4 3.1 %copy-start = (bf16[4,4,512,128]{3,2,1,0:T(8,128)(2,1)S(1)}, bf16[4,4,512,128]{3,2,1,0:T(8,128)(2,1)}, u32[]{:S(2)}) copy-start(bf16[4,4,512,128]{3,2,1,0:T(8,128)(2,1)} %get-tuple-element.21) | copy-start | bytes 6291460
